TPU v7x, 256 devices: a whole 4x4x8 slice. The times are simulated.
256 devices in a mesh: dp: 64 (over y, z, core), mp: 4 (over x).
Axes of the slice: x: 4, y: 4, z: 8, core: 2. Of those that a mesh axis runs over, the one named last changes fastest.
Arguments:
- cand_item: int32 [512, 128], P(('dp', 'mp')), may hold values from 0 to 131071, as said below
- list_place: int32 [512], replicated, may hold values from 0 to 511, as said below
- item_table: bfloat16 [131072, 768], P('dp', 'mp'), may hold values from -6 to 6
- query_vec: bfloat16 [512, 768], P(('dp', 'mp')), may hold values from -1.796875 to 1.796875
- labels: int32 [512, 128], P(('dp', 'mp')), may hold values from 0 to 4
- query_weight: bfloat16 [768, 768], replicated, may hold values from -0.75 to 0.75
- key_weight: bfloat16 [768, 768], replicated, may hold values from -0.75 to 0.75
- value_weight: bfloat16 [768, 768], replicated, may hold values from -0.21875 to 0.21875
- output_weight: bfloat16 [768, 768], replicated, may hold values from -0.21875 to 0.21875
- gain_attn: float32 [768], replicated, may hold values from 0.1 to 1.9
- gain_score: float32 [768], replicated, may hold values from 0.1 to 1.9
- w_score: float32 [768], replicated, may hold values from -0.6 to 0.6
Outputs:
- losses: float32 [512], P(('dp', 'mp'))
- table_grad: float32 [131072, 768], P('dp', 'mp')
- query_grad: float32 [512, 768], P(('dp', 'mp'))
- query_weight_gradient: float32 [768, 768], P('dp')
- key_weight_gradient: float32 [768, 768], P('dp')
- value_weight_gradient: float32 [768, 768], P('dp')
- output_weight_gradient: float32 [768, 768], P('dp')
- grad_gain_attn: float32 [768], replicated
- grad_gain_score: float32 [768], replicated
- grad_w_score: float32 [768], replicated
Inputs may be any that keep to these rules, and one draw needn't show every extreme that they name: `cand_item`: item i lies in list i // 256 at place i % 256. Of the 1024 candidates of the queries of one index of dp (aligned blocks of rows), at most 32 lie in lists stored on one index of dp; one index of dp, the same for every block, holds exactly 32 of the candidates of every block. A permutation: list l is stored as rows list_place[l] * 256 to list_place[l] * 256 + 255 of item_table.
All inputs are finite; a program needn't handle non-finite values.
Results may differ from a plain program's by a relative error of at most 0.025.
Values may be sent and summed in bfloat16 or wider, within the bound.
No kernel may reach another device: no remote copies, remote signals or barrier semaphores. Data moves between devices by JAX's collectives and lax.ppermute only.
A program may use at most 128 MiB of HBM per device.

v0:
```python
import jax
import jax.numpy as jnp
from jax import lax
from jax.sharding import PartitionSpec as P

HEADS = 12
LIST_LEN = 256


EPSILON = 1e-06
SCORE_CAP = 20.0
RANK_CAP = 30.0


def mixing_weights(form, left, right):
    return jnp.einsum(form, left, right, preferred_element_type=jnp.float32)


def layer_step(
    rows_in,
    query_vec,
    labels,
    query_weight,
    key_weight,
    value_weight,
    output_weight,
    gain_attn,
    gain_score,
    w_score,
):
    batch_size, set_size, width_all = rows_in.shape
    head_size = width_all // HEADS
    shrink = head_size ** (-0.5)
    base_scores = rows_in.astype(jnp.float32) + query_vec.astype(jnp.float32)[:, None, :]
    scale_one = jnp.sqrt(jnp.mean(base_scores * base_scores, -1, keepdims=True) + EPSILON)
    normed_one = base_scores / scale_one
    first_input = (normed_one * gain_attn).astype(jnp.bfloat16)
    projected_queries = mixing_weights("uvy,ym->uvm", first_input, query_weight).astype(
        jnp.bfloat16
    )
    projected_keys = mixing_weights("uvy,ym->uvm", first_input, key_weight).astype(jnp.bfloat16)
    projected_values = mixing_weights("uvy,ym->uvm", first_input, value_weight).astype(jnp.bfloat16)
    head_split_shape = (batch_size, set_size, HEADS, head_size)
    query_heads = projected_queries.reshape(head_split_shape)
    key_heads = projected_keys.reshape(head_split_shape)
    value_heads = projected_values.reshape(head_split_shape)
    logits = mixing_weights("bqhe,bkhe->bhqk", query_heads, key_heads) * shrink
    capped = SCORE_CAP * jnp.tanh(logits / SCORE_CAP)
    raised = jnp.exp(capped)
    attend = raised / jnp.sum(raised, -1, keepdims=True)
    attend_low = attend.astype(jnp.bfloat16)
    context_rows = (
        mixing_weights("bhqk,bkhe->bqhe", attend_low, value_heads)
        .astype(jnp.bfloat16)
        .reshape(batch_size, set_size, width_all)
    )
    mixed_output = base_scores + mixing_weights("uvy,ym->uvm", context_rows, output_weight)
    scale_two = jnp.sqrt(jnp.mean(mixed_output * mixed_output, -1, keepdims=True) + EPSILON)
    normed_two = mixed_output / scale_two
    scaled_two = normed_two * gain_score
    scores = RANK_CAP * jnp.tanh(jnp.sum(scaled_two * w_score, -1) / RANK_CAP)
    raised_scores = jnp.exp(scores)
    totals = jnp.sum(raised_scores, -1, keepdims=True)
    relevance = jnp.exp(labels.astype(jnp.float32))
    target = relevance / jnp.sum(relevance, -1, keepdims=True)
    losses = jnp.log(totals[:, 0]) - jnp.sum(target * scores, -1)
    diff_raw = (raised_scores / totals - target) * (1.0 - (scores / RANK_CAP) ** 2)
    grad_w_score = jnp.sum(scaled_two * diff_raw[..., None], (0, 1))
    diff_scaled = diff_raw[..., None] * w_score
    grad_gain_score = jnp.sum(normed_two * diff_scaled, (0, 1))
    diff_normed = diff_scaled * gain_score
    diff_mixed = (
        diff_normed - normed_two * jnp.mean(diff_normed * normed_two, -1, keepdims=True)
    ) / scale_two
    lower_gradient = diff_mixed.astype(jnp.bfloat16)
    output_weight_gradient = mixing_weights("fpg,fpi->gi", context_rows, lower_gradient)
    context_gradient = (
        mixing_weights("ifm,gm->ifg", lower_gradient, output_weight)
        .astype(jnp.bfloat16)
        .reshape(head_split_shape)
    )
    diff_attend = mixing_weights("bqhe,bkhe->bhqk", context_gradient, value_heads)
    value_gradient = mixing_weights("bhqk,bqhe->bkhe", attend_low, context_gradient).astype(
        jnp.bfloat16
    )
    diff_capped = attend * (diff_attend - jnp.sum(attend * diff_attend, -1, keepdims=True))
    diff_logits = (diff_capped * (1.0 - (capped / SCORE_CAP) ** 2) * shrink).astype(jnp.bfloat16)
    query_gradient = mixing_weights("bhqk,bkhe->bqhe", diff_logits, key_heads).astype(jnp.bfloat16)
    key_gradient = mixing_weights("bhqk,bqhe->bkhe", diff_logits, query_heads).astype(jnp.bfloat16)
    flat_shape = (batch_size, set_size, width_all)
    query_gradient = query_gradient.reshape(flat_shape)
    key_gradient = key_gradient.reshape(flat_shape)
    value_gradient = value_gradient.reshape(flat_shape)
    query_weight_gradient = mixing_weights("fpg,fpi->gi", first_input, query_gradient)
    key_weight_gradient = mixing_weights("fpg,fpi->gi", first_input, key_gradient)
    value_weight_gradient = mixing_weights("fpg,fpi->gi", first_input, value_gradient)
    input_gradient = (
        mixing_weights("ifm,gm->ifg", query_gradient, query_weight)
        + mixing_weights("ifm,gm->ifg", key_gradient, key_weight)
        + mixing_weights("ifm,gm->ifg", value_gradient, value_weight)
    )
    grad_gain_attn = jnp.sum(normed_one * input_gradient, (0, 1))
    diff_first = input_gradient * gain_attn
    diff_base = (
        diff_mixed
        + (diff_first - normed_one * jnp.mean(diff_first * normed_one, -1, keepdims=True))
        / scale_one
    )
    query_grad = jnp.sum(diff_base, 1)
    return (
        losses,
        diff_base,
        query_grad,
        (query_weight_gradient, key_weight_gradient, value_weight_gradient, output_weight_gradient),
        (grad_gain_attn, grad_gain_score, grad_w_score),
    )


def body(
    cand_item,
    list_place,
    item_table,
    query_vec,
    labels,
    query_weight,
    key_weight,
    value_weight,
    output_weight,
    gain_attn,
    gain_score,
    w_score,
):
    query_count, set_size = cand_item.shape
    rows_local = query_count * set_size
    dp_count = lax.axis_size("dp")
    mp_count = lax.axis_size("mp")
    group_rows = mp_count * rows_local
    capacity = 2 * group_rows // dp_count
    stored_rows, slab_width = item_table.shape
    lists_local = stored_rows // LIST_LEN
    group_items = lax.all_gather(cand_item.reshape(rows_local), "mp", axis=0, tiled=True)
    block_index = list_place[group_items // LIST_LEN]
    owner_index = block_index // lists_local
    local_row = block_index % lists_local * LIST_LEN + group_items % LIST_LEN
    onehot = (owner_index[:, None] == jnp.arange(dp_count, dtype=jnp.int32)[None, :]).astype(
        jnp.int32
    )
    position = jnp.sum((jnp.cumsum(onehot, 0) - onehot) * onehot, 1)
    slot_index = owner_index * capacity + position
    request = (
        jnp.full((dp_count * capacity,), -1, jnp.int32)
        .at[slot_index]
        .set(local_row)
        .reshape(dp_count, capacity)
    )
    asked_rows = lax.all_to_all(request, "dp", split_axis=0, concat_axis=0, tiled=True)
    looked = item_table[jnp.maximum(asked_rows, 0)]
    found = jnp.where((asked_rows >= 0)[..., None], looked, jnp.zeros((), jnp.bfloat16))
    flat_found = found.reshape(found.shape[0], found.shape[1] * found.shape[2])
    returned = lax.all_to_all(flat_found, "dp", split_axis=0, concat_axis=0, tiled=True)
    fetched, asked_rows = (returned.reshape(found.shape), asked_rows)
    slot_order = slot_index.reshape(mp_count, rows_local).T
    pieces = fetched.reshape(dp_count * capacity, slab_width)[slot_order]
    gathered_rows = lax.all_to_all(pieces, "mp", split_axis=1, concat_axis=1, tiled=True)
    rows_in = gathered_rows.reshape(query_count, set_size, mp_count * slab_width)
    losses, diff_base, query_grad, matrices, vectors = layer_step(
        rows_in,
        query_vec,
        labels,
        query_weight,
        key_weight,
        value_weight,
        output_weight,
        gain_attn,
        gain_score,
        w_score,
    )
    column_grads = lax.all_to_all(
        diff_base.reshape(rows_local, mp_count, slab_width).astype(jnp.bfloat16),
        "mp",
        split_axis=1,
        concat_axis=1,
        tiled=True,
    ).astype(jnp.float32)
    outgoing = (
        jnp.zeros((dp_count * capacity, slab_width), jnp.float32).at[slot_order].set(column_grads)
    )
    arrived = lax.all_to_all(
        outgoing.reshape(dp_count, capacity, slab_width).astype(jnp.bfloat16),
        "dp",
        split_axis=0,
        concat_axis=0,
        tiled=True,
    ).astype(jnp.float32)
    live = (asked_rows >= 0).reshape(dp_count * capacity, 1)
    landing = jnp.maximum(asked_rows, 0).reshape(dp_count * capacity)
    table_grad = (
        jnp.zeros((stored_rows, slab_width), jnp.float32)
        .at[landing]
        .add(jnp.where(live, arrived.reshape(dp_count * capacity, slab_width), 0.0))
    )
    slices = (
        lax.psum_scatter(matrices[0], "dp", scatter_dimension=0, tiled=True),
        lax.psum_scatter(matrices[1], "dp", scatter_dimension=0, tiled=True),
        lax.psum_scatter(matrices[2], "dp", scatter_dimension=0, tiled=True),
        lax.psum_scatter(matrices[3], "dp", scatter_dimension=0, tiled=True),
    )
    summed = (
        lax.psum(slices[0].astype(jnp.bfloat16), "mp").astype(jnp.float32),
        lax.psum(slices[1].astype(jnp.bfloat16), "mp").astype(jnp.float32),
        lax.psum(slices[2].astype(jnp.bfloat16), "mp").astype(jnp.float32),
        lax.psum(slices[3].astype(jnp.bfloat16), "mp").astype(jnp.float32),
    )
    vector_totals = lax.psum((vectors[0], vectors[1], vectors[2]), ("dp", "mp"))
    return (
        losses,
        table_grad,
        query_grad,
        summed[0],
        summed[1],
        summed[2],
        summed[3],
        vector_totals[0],
        vector_totals[1],
        vector_totals[2],
    )


def solution(mesh):
    placed = (
        P(("dp", "mp"), None),
        P(),
        P("dp", "mp"),
        P(("dp", "mp"), None),
        P(("dp", "mp"), None),
        P(),
        P(),
        P(),
        P(),
        P(),
        P(),
        P(),
    )
    return jax.shard_map(
        body,
        mesh=mesh,
        in_specs=placed,
        out_specs=(
            P(("dp", "mp")),
            P("dp", "mp"),
            P(("dp", "mp"), None),
            P("dp", None),
            P("dp", None),
            P("dp", None),
            P("dp", None),
            P(),
            P(),
            P(),
        ),
        check_vma=False,
    )
```

profile of v0, /device:TPU:1, one launch (start us, length us, event | category | flops | bytes accessed | tf_op | source)
XLA Modules:
  0.0 671.7 jit_solution(3605366448102224969)
XLA Ops:
  7.2 8.9 %all-gather = s32[4,1,256]{2,1,0:T(1,128)S(1)} all-gather(s32[1,1,256]{2,1,0:T(1,128)} %bitcast.169), channel_id=1, replica_groups=mesh['dp'=64,'mp'=4] {'mp'}, dimensions={0}, use_global_device_ids=true | all-gather | bytes 5120 | tf_op jit(solution)/shard_map/all_gather | solution.py:141
  16.1 6.9 %gather_fusion = s32[1024]{0:T(1024)S(1)} fusion(s32[512]{0:T(512)S(1)} %copy-done.1, s32[1024]{0:T(1024)S(1)} %fusion.54), kind=kCustom, calls=%fused_computation | custom fusion | bytes 12288 | tf_op jit(solution)/shard_map/gather | solution.py:142
  23.1 18.0 %reduce-window.6 = s32[64,8,128]{2,1,0:T(8,128)S(1)} reduce-window(s32[64,8,128]{2,1,0:T(8,128)S(1)} %fusion.44, s32[]{:T(128)} %constant.81.clone.1), window={size=1x1x128 pad=0_0x0_0x127_0}, to_apply=%region_0.1 | reduce-window | flops 8323072 | bytes 524292 | tf_op jit(solution)/shard_map/reduce-window
  41.8 4.3 scatter_custom_fusion
  46.8 14.3 %all-to-all-start = ((s32[64,1,32]{2,1,0:T(1,128)}), s32[64,1,32]{2,1,0:T(1,128)S(1)}, u32[]{:S(2)}, u32[]{:S(2)}) async-start(s32[64,1,32]{2,1,0:T(1,128)} %bitcast.8), calls=%async_computation | async-start | bytes 65536 | tf_op jit(solution)/shard_map/all_to_all | solution.py:156
  61.7 8.7 %all-to-all-done = s32[64,1,32]{2,1,0:T(1,128)S(1)} async-done(((s32[64,1,32]{2,1,0:T(1,128)}), s32[64,1,32]{2,1,0:T(1,128)S(1)}, u32[]{:S(2)}, u32[]{:S(2)}) %all-to-all-start) | async-done | bytes 8224 | tf_op jit(solution)/shard_map/all_to_all | solution.py:156
  71.0 7.5 %gather_fusion.1 = bf16[2048,192]{1,0:T(8,128)(2,1)S(1)} fusion(bf16[2048,192]{1,0:T(8,128)(2,1)S(1)} %copy.138, s32[2048]{0:T(1024)S(1)} %broadcast_clamp_fusion), kind=kCustom, calls=%fused_computation.1 | custom fusion | bytes 1581056 | tf_op jit(solution)/shard_map/gather | solution.py:157
  79.8 4.8 select_n.89
  85.1 5.4 reduce.2
  91.9 5.3 all-to-all-start.1
  98.2 22.1 %all-to-all-done.1 = bf16[64,2,3072]{2,1,0:T(2,128)(2,1)S(1)} async-done(((bf16[64,2,3072]{2,1,0:T(2,128)(2,1)}), bf16[64,2,3072]{2,1,0:T(2,128)(2,1)S(1)}, u32[]{:S(2)}, u32[]{:S(2)}) %all-to-all-start.1) | async-done | bytes 786464 | tf_op jit(solution)/shard_map/all_to_all | solution.py:160
  120.9 4.7 reduce.1
  126.8 3.9 gather_fusion.2
  132.0 3.5 all-to-all-start.2
  138.6 4.6 all-to-all-done.2
  163.8 3.0 convolution_convert_fusion
  168.4 4.8 convolution_convert_fusion.2
  173.2 4.8 convolution_convert_fusion.1
  178.0 1.9 multiply_convert_fusion.1
  181.1 2.0 fusion.14
  185.0 2.0 convolution_bitcast_fusion.2
  193.8 3.7 all-to-all-start.3
  197.5 2.1 convolution_bitcast_fusion
  199.6 4.4 all-to-all-done.3
  204.6 6.3 scatter_custom_fusion.1
  210.9 2.8 convert_element_type.146
  213.7 8.6 %all-to-all-start.4 = ((bf16[64,32,192]{2,1,0:T(8,128)(2,1)}), bf16[64,32,192]{2,1,0:T(8,128)(2,1)}, u32[]{:S(2)}, u32[]{:S(2)}) async-start(bf16[64,32,192]{2,1,0:T(8,128)(2,1)} %bitcast.144), calls=%async_computation.4 | async-start | bytes 2097152 | tf_op jit(solution)/shard_map/all_to_all | solution.py:188
  222.4 167.4 %fusion.82 = (f32[16,768]{1,0:T(8,128)}, f32[16,768]{1,0:T(8,128)}, f32[16,768]{1,0:T(8,128)}, f32[16,768]{1,0:T(8,128)}) fusion(f32[768,768]{1,0:T(8,128)S(1)} %copy-done.2, f32[768,768]{1,0:T(8,128)} %convolution_bitcast_fusion.2, f32[768,768]{1,0:T(8,128)} %convolution_bitcast_fusion.1, f32[768,768]{1,0:T(8,128)} %convolution_bitcast_fusion), kind=kCustom, calls=%all-reduce-scatter.4 | all-reduce-scatter fusion | flops 3145729 | bytes 9634816
  403.0 12.0 %collective-permute-start.52 = (bf16[16,768]{1,0:T(8,128)(2,1)S(1)}, bf16[16,768]{1,0:T(8,128)(2,1)S(1)}, u32[]{:S(2)}, u32[]{:S(2)}) collective-permute-start(bf16[16,768]{1,0:T(8,128)(2,1)S(1)} %convert.128), channel_id=1, source_target_pairs={{0,20},{4,24},{8,28},{12,32},{16,36},{20,40},{24,44},{28,48},{32,5... | collective-permute-start | bytes 73736
  416.4 2.2 collective-permute-start.54
  418.7 7.6 %collective-permute-start.55 = (bf16[16,768]{1,0:T(8,128)(2,1)S(1)}, bf16[16,768]{1,0:T(8,128)(2,1)S(1)}, u32[]{:S(2)}, u32[]{:S(2)}) collective-permute-start(bf16[16,768]{1,0:T(8,128)(2,1)S(1)} %convert.128), channel_id=1, source_target_pairs={{0,32},{4,36},{8,40},{12,44},{16,48},{20,52},{24,56},{28,60},{32,6... | collective-permute-start | bytes 73736
  427.5 5.8 collective-permute-start.57
  433.4 3.0 collective-permute-start.58
  441.8 2.7 collective-permute-start.48
  445.3 2.8 collective-permute-start.33
  450.0 3.5 collective-permute-start.35
  453.5 5.2 collective-permute-start.36
  458.7 2.2 collective-permute-start.37
  460.9 2.8 collective-permute-start.38
  463.7 2.5 collective-permute-start.39
  466.2 2.1 collective-permute-start.40
  474.3 2.2 collective-permute-start.45
  477.8 2.2 collective-permute-start.32
  482.6 2.4 collective-permute-start.18
  485.0 4.5 collective-permute-start.19
  489.5 4.7 collective-permute-start.20
  495.7 2.2 collective-permute-start.22
  497.9 2.0 collective-permute-start.23
  506.7 2.2 collective-permute-start.29
  510.2 2.1 collective-permute-start.16
  513.1 2.2 collective-permute-start.1
  515.3 2.3 collective-permute-start.2
  517.6 4.7 collective-permute-start.3
  522.4 4.6 collective-permute-start.4
  528.5 2.1 collective-permute-start.6
  538.4 2.0 collective-permute-start.11
  546.1 2.7 collective-permute-start
  549.1 3.2 concatenate.3
  552.4 3.0 concatenate.2
  555.4 2.2 concatenate.1
  557.7 7.8 %concatenate = bf16[268,768]{1,0:T(8,128)(2,1)S(1)} concatenate(bf16[12,768]{1,0:T(8,128)(2,1)S(1)} %collective-permute-done.15, bf16[16,768]{1,0:T(8,128)(2,1)} %collective-permute-done.14, bf16[16,768]{1,0:T(8,128)(2,1)} %collective-permute-done.13, bf16[16,768]{1,0:T(8,128)(2,1)} %collective-permute-done.12, bf16[16,768]{1,0:T(8,128)(2,1)} %collective-permute-done.11, ...), dimensions={0} | concatenate | bytes 847872
  568.6 73.1 %all-reduce.8 = (f32[768]{0:T(1024)}, f32[768]{0:T(1024)}, f32[768]{0:T(1024)}) all-reduce(f32[768]{0:T(1024)S(1)} %copy-done.46, f32[768]{0:T(1024)S(1)} %copy-done.35, f32[768]{0:T(1024)S(1)} %copy-done.34), channel_id=1, replica_groups=mesh['dp'=64,'mp'=4] {'dp','mp'}, use_global_device_ids=true, to_apply=%region_26.27 | all-reduce | flops 2304 | bytes 18432 | tf_op jit(solution)/shard_map/psum | solution.py:214
  647.2 2.9 convert_select_fusion
  650.1 12.6 %scatter_custom_fusion.2 = f32[2048,192]{1,0:T(8,128)S(1)} fusion(s32[2048]{0:T(1024)} %copy-done.23, f32[2048,192]{1,0:T(8,128)} %convert_select_fusion, f32[]{:T(128)} %constant.91.clone.1), kind=kCustom, calls=%fused_computation.43 | custom fusion | flops 393216 | bytes 1573376 | tf_op jit(solution)/shard_map/scatter-add | solution.py:200
  (309 shorter events, 113.6 us)
Async XLA Ops:
  46.8 23.6 %all-to-all-start = ((s32[64,1,32]{2,1,0:T(1,128)}), s32[64,1,32]{2,1,0:T(1,128)S(1)}, u32[]{:S(2)}, u32[]{:S(2)}) async-start(s32[64,1,32]{2,1,0:T(1,128)} %bitcast.8), calls=%async_computation | async-start | bytes 65536 | tf_op jit(solution)/shard_map/all_to_all | solution.py:156
  91.9 28.3 %all-to-all-start.1 = ((bf16[64,2,3072]{2,1,0:T(2,128)(2,1)}), bf16[64,2,3072]{2,1,0:T(2,128)(2,1)S(1)}, u32[]{:S(2)}, u32[]{:S(2)}) async-start(bf16[64,2,3072]{2,1,0:T(2,128)(2,1)} %reshape.371), calls=%async_computation.1 | async-start | bytes 1572864 | tf_op jit(solution)/shard_map/all_to_all | solution.py:160
  132.0 11.2 %all-to-all-start.2 = ((bf16[256,4,192]{0,2,1:T(8,128)(2,1)}), bf16[256,4,192]{0,2,1:T(8,128)(2,1)S(1)}, u32[]{:S(2)}, u32[]{:S(2)}) async-start(bf16[256,4,192]{0,2,1:T(8,128)(2,1)} %copy.141), calls=%async_computation.2 | async-start | bytes 786432 | tf_op jit(solution)/shard_map/all_to_all | solution.py:164
  193.8 10.2 %all-to-all-start.3 = ((bf16[256,4,192]{0,2,1:T(8,128)(2,1)}), bf16[256,4,192]{0,2,1:T(8,128)(2,1)S(1)}, u32[]{:S(2)}, u32[]{:S(2)}) async-start(bf16[256,4,192]{0,2,1:T(8,128)(2,1)} %convert_element_type.144), calls=%async_computation.3 | async-start | bytes 786432 | tf_op jit(solution)/shard_map/all_to_all | solution.py:178
  213.7 433.4 %all-to-all-start.4 = ((bf16[64,32,192]{2,1,0:T(8,128)(2,1)}), bf16[64,32,192]{2,1,0:T(8,128)(2,1)}, u32[]{:S(2)}, u32[]{:S(2)}) async-start(bf16[64,32,192]{2,1,0:T(8,128)(2,1)} %bitcast.144), calls=%async_computation.4 | async-start | bytes 2097152 | tf_op jit(solution)/shard_map/all_to_all | solution.py:188
  222.4 419.3 %all-reduce.13.cloned.1.call-start = ((), (), s32[]{:S(2)}) async-start(), calls=%async_computation.5 | async-start | bytes 196608 | tf_op jit(solution)/shard_map/psum | solution.py:209
  391.6 8.9 %collective-permute-start.63 = (bf16[12,768]{1,0:T(8,128)(2,1)S(1)}, bf16[12,768]{1,0:T(8,128)(2,1)S(1)}, u32[]{:S(2)}, u32[]{:S(2)}) collective-permute-start(bf16[12,768]{1,0:T(8,128)(2,1)S(1)} %slice.19), channel_id=1, source_target_pairs={{0,64},{4,68},{8,72},{12,76},{16,80},{20,84},{24,88},{28,92},{32,9... | collective-permute-start | bytes 55304
  393.6 8.1 %collective-permute-start.47 = (bf16[12,768]{1,0:T(8,128)(2,1)S(1)}, bf16[12,768]{1,0:T(8,128)(2,1)S(1)}, u32[]{:S(2)}, u32[]{:S(2)}) collective-permute-start(bf16[12,768]{1,0:T(8,128)(2,1)S(1)} %slice.18), channel_id=1, source_target_pairs={{0,64},{4,68},{8,72},{12,76},{16,80},{20,84},{24,88},{28,92},{32,9... | collective-permute-start | bytes 55304
  394.9 8.1 %collective-permute-start.31 = (bf16[12,768]{1,0:T(8,128)(2,1)S(1)}, bf16[12,768]{1,0:T(8,128)(2,1)S(1)}, u32[]{:S(2)}, u32[]{:S(2)}) collective-permute-start(bf16[12,768]{1,0:T(8,128)(2,1)S(1)} %slice.17), channel_id=1, source_target_pairs={{0,64},{4,68},{8,72},{12,76},{16,80},{20,84},{24,88},{28,92},{32,9... | collective-permute-start | bytes 55304
  397.0 18.0 %collective-permute-start.15 = (bf16[12,768]{1,0:T(8,128)(2,1)S(1)}, bf16[12,768]{1,0:T(8,128)(2,1)S(1)}, u32[]{:S(2)}, u32[]{:S(2)}) collective-permute-start(bf16[12,768]{1,0:T(8,128)(2,1)S(1)} %slice.16), channel_id=1, source_target_pairs={{0,64},{4,68},{8,72},{12,76},{16,80},{20,84},{24,88},{28,92},{32,9... | collective-permute-start | bytes 55304
  399.1 17.3 %collective-permute-start.49 = (bf16[16,768]{1,0:T(8,128)(2,1)S(1)}, bf16[16,768]{1,0:T(8,128)(2,1)S(1)}, u32[]{:S(2)}, u32[]{:S(2)}) collective-permute-start(bf16[16,768]{1,0:T(8,128)(2,1)S(1)} %convert.128), channel_id=1, source_target_pairs={{0,8},{4,12},{8,16},{12,20},{16,24},{20,28},{24,32},{28,36},{32,40... | collective-permute-start | bytes 73736
  400.4 18.2 %collective-permute-start.50 = (bf16[16,768]{1,0:T(8,128)(2,1)S(1)}, bf16[16,768]{1,0:T(8,128)(2,1)S(1)}, u32[]{:S(2)}, u32[]{:S(2)}) collective-permute-start(bf16[16,768]{1,0:T(8,128)(2,1)S(1)} %convert.128), channel_id=1, source_target_pairs={{0,12},{4,16},{8,20},{12,24},{16,28},{20,32},{24,36},{28,40},{32,4... | collective-permute-start | bytes 73736
  401.7 24.5 %collective-permute-start.51 = (bf16[16,768]{1,0:T(8,128)(2,1)S(1)}, bf16[16,768]{1,0:T(8,128)(2,1)S(1)}, u32[]{:S(2)}, u32[]{:S(2)}) collective-permute-start(bf16[16,768]{1,0:T(8,128)(2,1)S(1)} %convert.128), channel_id=1, source_target_pairs={{0,16},{4,20},{8,24},{12,28},{16,32},{20,36},{24,40},{28,44},{32,4... | collective-permute-start | bytes 73736
  403.0 24.5 %collective-permute-start.52 = (bf16[16,768]{1,0:T(8,128)(2,1)S(1)}, bf16[16,768]{1,0:T(8,128)(2,1)S(1)}, u32[]{:S(2)}, u32[]{:S(2)}) collective-permute-start(bf16[16,768]{1,0:T(8,128)(2,1)S(1)} %convert.128), channel_id=1, source_target_pairs={{0,20},{4,24},{8,28},{12,32},{16,36},{20,40},{24,44},{28,48},{32,5... | collective-permute-start | bytes 73736
  415.1 18.3 %collective-permute-start.53 = (bf16[16,768]{1,0:T(8,128)(2,1)S(1)}, bf16[16,768]{1,0:T(8,128)(2,1)S(1)}, u32[]{:S(2)}, u32[]{:S(2)}) collective-permute-start(bf16[16,768]{1,0:T(8,128)(2,1)S(1)} %convert.128), channel_id=1, source_target_pairs={{0,24},{4,28},{8,32},{12,36},{16,40},{20,44},{24,48},{28,52},{32,5... | collective-permute-start | bytes 73736
  416.4 19.9 %collective-permute-start.54 = (bf16[16,768]{1,0:T(8,128)(2,1)S(1)}, bf16[16,768]{1,0:T(8,128)(2,1)S(1)}, u32[]{:S(2)}, u32[]{:S(2)}) collective-permute-start(bf16[16,768]{1,0:T(8,128)(2,1)S(1)} %convert.128), channel_id=1, source_target_pairs={{0,28},{4,32},{8,36},{12,40},{16,44},{20,48},{24,52},{28,56},{32,6... | collective-permute-start | bytes 73736
  418.7 19.0 %collective-permute-start.55 = (bf16[16,768]{1,0:T(8,128)(2,1)S(1)}, bf16[16,768]{1,0:T(8,128)(2,1)S(1)}, u32[]{:S(2)}, u32[]{:S(2)}) collective-permute-start(bf16[16,768]{1,0:T(8,128)(2,1)S(1)} %convert.128), channel_id=1, source_target_pairs={{0,32},{4,36},{8,40},{12,44},{16,48},{20,52},{24,56},{28,60},{32,6... | collective-permute-start | bytes 73736
  426.2 12.8 %collective-permute-start.56 = (bf16[16,768]{1,0:T(8,128)(2,1)S(1)}, bf16[16,768]{1,0:T(8,128)(2,1)S(1)}, u32[]{:S(2)}, u32[]{:S(2)}) collective-permute-start(bf16[16,768]{1,0:T(8,128)(2,1)S(1)} %convert.128), channel_id=1, source_target_pairs={{0,36},{4,40},{8,44},{12,48},{16,52},{20,56},{24,60},{28,64},{32,6... | collective-permute-start | bytes 73736
  427.5 12.8 %collective-permute-start.57 = (bf16[16,768]{1,0:T(8,128)(2,1)S(1)}, bf16[16,768]{1,0:T(8,128)(2,1)S(1)}, u32[]{:S(2)}, u32[]{:S(2)}) collective-permute-start(bf16[16,768]{1,0:T(8,128)(2,1)S(1)} %convert.128), channel_id=1, source_target_pairs={{0,40},{4,44},{8,48},{12,52},{16,56},{20,60},{24,64},{28,68},{32,7... | collective-permute-start | bytes 73736
  433.4 8.3 %collective-permute-start.58 = (bf16[16,768]{1,0:T(8,128)(2,1)S(1)}, bf16[16,768]{1,0:T(8,128)(2,1)S(1)}, u32[]{:S(2)}, u32[]{:S(2)}) collective-permute-start(bf16[16,768]{1,0:T(8,128)(2,1)S(1)} %convert.128), channel_id=1, source_target_pairs={{0,44},{4,48},{8,52},{12,56},{16,60},{20,64},{24,68},{28,72},{32,7... | collective-permute-start | bytes 73736
  436.4 8.9 %collective-permute-start.59 = (bf16[16,768]{1,0:T(8,128)(2,1)S(1)}, bf16[16,768]{1,0:T(8,128)(2,1)S(1)}, u32[]{:S(2)}, u32[]{:S(2)}) collective-permute-start(bf16[16,768]{1,0:T(8,128)(2,1)S(1)} %convert.128), channel_id=1, source_target_pairs={{0,48},{4,52},{8,56},{12,60},{16,64},{20,68},{24,72},{28,76},{32,8... | collective-permute-start | bytes 73736
  437.7 10.4 %collective-permute-start.60 = (bf16[16,768]{1,0:T(8,128)(2,1)S(1)}, bf16[16,768]{1,0:T(8,128)(2,1)S(1)}, u32[]{:S(2)}, u32[]{:S(2)}) collective-permute-start(bf16[16,768]{1,0:T(8,128)(2,1)S(1)} %convert.128), channel_id=1, source_target_pairs={{0,52},{4,56},{8,60},{12,64},{16,68},{20,72},{24,76},{28,80},{32,8... | collective-permute-start | bytes 73736
  439.1 10.9 %collective-permute-start.61 = (bf16[16,768]{1,0:T(8,128)(2,1)S(1)}, bf16[16,768]{1,0:T(8,128)(2,1)S(1)}, u32[]{:S(2)}, u32[]{:S(2)}) collective-permute-start(bf16[16,768]{1,0:T(8,128)(2,1)S(1)} %convert.128), channel_id=1, source_target_pairs={{0,56},{4,60},{8,64},{12,68},{16,72},{20,76},{24,80},{28,84},{32,8... | collective-permute-start | bytes 73736
  440.4 13.1 %collective-permute-start.62 = (bf16[16,768]{1,0:T(8,128)(2,1)S(1)}, bf16[16,768]{1,0:T(8,128)(2,1)S(1)}, u32[]{:S(2)}, u32[]{:S(2)}) collective-permute-start(bf16[16,768]{1,0:T(8,128)(2,1)S(1)} %convert.128), channel_id=1, source_target_pairs={{0,60},{4,64},{8,68},{12,72},{16,76},{20,80},{24,84},{28,88},{32,9... | collective-permute-start | bytes 73736
  441.8 16.9 %collective-permute-start.48 = (bf16[16,768]{1,0:T(8,128)(2,1)S(1)}, bf16[16,768]{1,0:T(8,128)(2,1)S(1)}, u32[]{:S(2)}, u32[]{:S(2)}) collective-permute-start(bf16[16,768]{1,0:T(8,128)(2,1)S(1)} %convert.128), channel_id=1, source_target_pairs={{0,4},{4,8},{8,12},{12,16},{16,20},{20,24},{24,28},{28,32},{32,36}... | collective-permute-start | bytes 73736
  445.3 15.6 %collective-permute-start.33 = (bf16[16,768]{1,0:T(8,128)(2,1)S(1)}, bf16[16,768]{1,0:T(8,128)(2,1)S(1)}, u32[]{:S(2)}, u32[]{:S(2)}) collective-permute-start(bf16[16,768]{1,0:T(8,128)(2,1)S(1)} %convert.129), channel_id=1, source_target_pairs={{0,8},{4,12},{8,16},{12,20},{16,24},{20,28},{24,32},{28,36},{32,40... | collective-permute-start | bytes 73736
  448.1 15.6 %collective-permute-start.34 = (bf16[16,768]{1,0:T(8,128)(2,1)S(1)}, bf16[16,768]{1,0:T(8,128)(2,1)S(1)}, u32[]{:S(2)}, u32[]{:S(2)}) collective-permute-start(bf16[16,768]{1,0:T(8,128)(2,1)S(1)} %convert.129), channel_id=1, source_target_pairs={{0,12},{4,16},{8,20},{12,24},{16,28},{20,32},{24,36},{28,40},{32,4... | collective-permute-start | bytes 73736
  450.0 16.2 %collective-permute-start.35 = (bf16[16,768]{1,0:T(8,128)(2,1)S(1)}, bf16[16,768]{1,0:T(8,128)(2,1)S(1)}, u32[]{:S(2)}, u32[]{:S(2)}) collective-permute-start(bf16[16,768]{1,0:T(8,128)(2,1)S(1)} %convert.129), channel_id=1, source_target_pairs={{0,16},{4,20},{8,24},{12,28},{16,32},{20,36},{24,40},{28,44},{32,4... | collective-permute-start | bytes 73736
  453.5 14.8 %collective-permute-start.36 = (bf16[16,768]{1,0:T(8,128)(2,1)S(1)}, bf16[16,768]{1,0:T(8,128)(2,1)S(1)}, u32[]{:S(2)}, u32[]{:S(2)}) collective-permute-start(bf16[16,768]{1,0:T(8,128)(2,1)S(1)} %convert.129), channel_id=1, source_target_pairs={{0,20},{4,24},{8,28},{12,32},{16,36},{20,40},{24,44},{28,48},{32,5... | collective-permute-start | bytes 73736
  458.7 11.3 %collective-permute-start.37 = (bf16[16,768]{1,0:T(8,128)(2,1)S(1)}, bf16[16,768]{1,0:T(8,128)(2,1)S(1)}, u32[]{:S(2)}, u32[]{:S(2)}) collective-permute-start(bf16[16,768]{1,0:T(8,128)(2,1)S(1)} %convert.129), channel_id=1, source_target_pairs={{0,24},{4,28},{8,32},{12,36},{16,40},{20,44},{24,48},{28,52},{32,5... | collective-permute-start | bytes 73736
  460.9 10.4 %collective-permute-start.38 = (bf16[16,768]{1,0:T(8,128)(2,1)S(1)}, bf16[16,768]{1,0:T(8,128)(2,1)S(1)}, u32[]{:S(2)}, u32[]{:S(2)}) collective-permute-start(bf16[16,768]{1,0:T(8,128)(2,1)S(1)} %convert.129), channel_id=1, source_target_pairs={{0,28},{4,32},{8,36},{12,40},{16,44},{20,48},{24,52},{28,56},{32,6... | collective-permute-start | bytes 73736
  463.7 8.9 %collective-permute-start.39 = (bf16[16,768]{1,0:T(8,128)(2,1)S(1)}, bf16[16,768]{1,0:T(8,128)(2,1)S(1)}, u32[]{:S(2)}, u32[]{:S(2)}) collective-permute-start(bf16[16,768]{1,0:T(8,128)(2,1)S(1)} %convert.129), channel_id=1, source_target_pairs={{0,32},{4,36},{8,40},{12,44},{16,48},{20,52},{24,56},{28,60},{32,6... | collective-permute-start | bytes 73736
  468.3 8.2 %collective-permute-start.41 = (bf16[16,768]{1,0:T(8,128)(2,1)S(1)}, bf16[16,768]{1,0:T(8,128)(2,1)S(1)}, u32[]{:S(2)}, u32[]{:S(2)}) collective-permute-start(bf16[16,768]{1,0:T(8,128)(2,1)S(1)} %convert.129), channel_id=1, source_target_pairs={{0,40},{4,44},{8,48},{12,52},{16,56},{20,60},{24,64},{28,68},{32,7... | collective-permute-start | bytes 73736
  471.3 9.5 %collective-permute-start.43 = (bf16[16,768]{1,0:T(8,128)(2,1)S(1)}, bf16[16,768]{1,0:T(8,128)(2,1)S(1)}, u32[]{:S(2)}, u32[]{:S(2)}) collective-permute-start(bf16[16,768]{1,0:T(8,128)(2,1)S(1)} %convert.129), channel_id=1, source_target_pairs={{0,48},{4,52},{8,56},{12,60},{16,64},{20,68},{24,72},{28,76},{32,8... | collective-permute-start | bytes 73736
  472.7 10.0 %collective-permute-start.44 = (bf16[16,768]{1,0:T(8,128)(2,1)S(1)}, bf16[16,768]{1,0:T(8,128)(2,1)S(1)}, u32[]{:S(2)}, u32[]{:S(2)}) collective-permute-start(bf16[16,768]{1,0:T(8,128)(2,1)S(1)} %convert.129), channel_id=1, source_target_pairs={{0,52},{4,56},{8,60},{12,64},{16,68},{20,72},{24,76},{28,80},{32,8... | collective-permute-start | bytes 73736
  474.3 10.7 %collective-permute-start.45 = (bf16[16,768]{1,0:T(8,128)(2,1)S(1)}, bf16[16,768]{1,0:T(8,128)(2,1)S(1)}, u32[]{:S(2)}, u32[]{:S(2)}) collective-permute-start(bf16[16,768]{1,0:T(8,128)(2,1)S(1)} %convert.129), channel_id=1, source_target_pairs={{0,56},{4,60},{8,64},{12,68},{16,72},{20,76},{24,80},{28,84},{32,8... | collective-permute-start | bytes 73736
  476.5 13.0 %collective-permute-start.46 = (bf16[16,768]{1,0:T(8,128)(2,1)S(1)}, bf16[16,768]{1,0:T(8,128)(2,1)S(1)}, u32[]{:S(2)}, u32[]{:S(2)}) collective-permute-start(bf16[16,768]{1,0:T(8,128)(2,1)S(1)} %convert.129), channel_id=1, source_target_pairs={{0,60},{4,64},{8,68},{12,72},{16,76},{20,80},{24,84},{28,88},{32,9... | collective-permute-start | bytes 73736
  477.8 16.5 %collective-permute-start.32 = (bf16[16,768]{1,0:T(8,128)(2,1)S(1)}, bf16[16,768]{1,0:T(8,128)(2,1)S(1)}, u32[]{:S(2)}, u32[]{:S(2)}) collective-permute-start(bf16[16,768]{1,0:T(8,128)(2,1)S(1)} %convert.129), channel_id=1, source_target_pairs={{0,4},{4,8},{8,12},{12,16},{16,20},{20,24},{24,28},{28,32},{32,36}... | collective-permute-start | bytes 73736
  480.8 14.9 %collective-permute-start.17 = (bf16[16,768]{1,0:T(8,128)(2,1)S(1)}, bf16[16,768]{1,0:T(8,128)(2,1)S(1)}, u32[]{:S(2)}, u32[]{:S(2)}) collective-permute-start(bf16[16,768]{1,0:T(8,128)(2,1)S(1)} %convert.130), channel_id=1, source_target_pairs={{0,8},{4,12},{8,16},{12,20},{16,24},{20,28},{24,32},{28,36},{32,40... | collective-permute-start | bytes 73736
  482.6 15.2 %collective-permute-start.18 = (bf16[16,768]{1,0:T(8,128)(2,1)S(1)}, bf16[16,768]{1,0:T(8,128)(2,1)S(1)}, u32[]{:S(2)}, u32[]{:S(2)}) collective-permute-start(bf16[16,768]{1,0:T(8,128)(2,1)S(1)} %convert.130), channel_id=1, source_target_pairs={{0,12},{4,16},{8,20},{12,24},{16,28},{20,32},{24,36},{28,40},{32,4... | collective-permute-start | bytes 73736
  485.0 14.8 %collective-permute-start.19 = (bf16[16,768]{1,0:T(8,128)(2,1)S(1)}, bf16[16,768]{1,0:T(8,128)(2,1)S(1)}, u32[]{:S(2)}, u32[]{:S(2)}) collective-permute-start(bf16[16,768]{1,0:T(8,128)(2,1)S(1)} %convert.130), channel_id=1, source_target_pairs={{0,16},{4,20},{8,24},{12,28},{16,32},{20,36},{24,40},{28,44},{32,4... | collective-permute-start | bytes 73736
  489.5 11.6 %collective-permute-start.20 = (bf16[16,768]{1,0:T(8,128)(2,1)S(1)}, bf16[16,768]{1,0:T(8,128)(2,1)S(1)}, u32[]{:S(2)}, u32[]{:S(2)}) collective-permute-start(bf16[16,768]{1,0:T(8,128)(2,1)S(1)} %convert.130), channel_id=1, source_target_pairs={{0,20},{4,24},{8,28},{12,32},{16,36},{20,40},{24,44},{28,48},{32,5... | collective-permute-start | bytes 73736
  494.3 8.3 %collective-permute-start.21 = (bf16[16,768]{1,0:T(8,128)(2,1)S(1)}, bf16[16,768]{1,0:T(8,128)(2,1)S(1)}, u32[]{:S(2)}, u32[]{:S(2)}) collective-permute-start(bf16[16,768]{1,0:T(8,128)(2,1)S(1)} %convert.130), channel_id=1, source_target_pairs={{0,24},{4,28},{8,32},{12,36},{16,40},{20,44},{24,48},{28,52},{32,5... | collective-permute-start | bytes 73736
  495.7 8.2 %collective-permute-start.22 = (bf16[16,768]{1,0:T(8,128)(2,1)S(1)}, bf16[16,768]{1,0:T(8,128)(2,1)S(1)}, u32[]{:S(2)}, u32[]{:S(2)}) collective-permute-start(bf16[16,768]{1,0:T(8,128)(2,1)S(1)} %convert.130), channel_id=1, source_target_pairs={{0,28},{4,32},{8,36},{12,40},{16,44},{20,48},{24,52},{28,56},{32,6... | collective-permute-start | bytes 73736
  503.9 9.2 %collective-permute-start.27 = (bf16[16,768]{1,0:T(8,128)(2,1)S(1)}, bf16[16,768]{1,0:T(8,128)(2,1)S(1)}, u32[]{:S(2)}, u32[]{:S(2)}) collective-permute-start(bf16[16,768]{1,0:T(8,128)(2,1)S(1)} %convert.130), channel_id=1, source_target_pairs={{0,48},{4,52},{8,56},{12,60},{16,64},{20,68},{24,72},{28,76},{32,8... | collective-permute-start | bytes 73736
  505.3 10.0 %collective-permute-start.28 = (bf16[16,768]{1,0:T(8,128)(2,1)S(1)}, bf16[16,768]{1,0:T(8,128)(2,1)S(1)}, u32[]{:S(2)}, u32[]{:S(2)}) collective-permute-start(bf16[16,768]{1,0:T(8,128)(2,1)S(1)} %convert.130), channel_id=1, source_target_pairs={{0,52},{4,56},{8,60},{12,64},{16,68},{20,72},{24,76},{28,80},{32,8... | collective-permute-start | bytes 73736
  506.7 11.0 %collective-permute-start.29 = (bf16[16,768]{1,0:T(8,128)(2,1)S(1)}, bf16[16,768]{1,0:T(8,128)(2,1)S(1)}, u32[]{:S(2)}, u32[]{:S(2)}) collective-permute-start(bf16[16,768]{1,0:T(8,128)(2,1)S(1)} %convert.130), channel_id=1, source_target_pairs={{0,56},{4,60},{8,64},{12,68},{16,72},{20,76},{24,80},{28,84},{32,8... | collective-permute-start | bytes 73736
  508.9 13.5 %collective-permute-start.30 = (bf16[16,768]{1,0:T(8,128)(2,1)S(1)}, bf16[16,768]{1,0:T(8,128)(2,1)S(1)}, u32[]{:S(2)}, u32[]{:S(2)}) collective-permute-start(bf16[16,768]{1,0:T(8,128)(2,1)S(1)} %convert.130), channel_id=1, source_target_pairs={{0,60},{4,64},{8,68},{12,72},{16,76},{20,80},{24,84},{28,88},{32,9... | collective-permute-start | bytes 73736
  510.2 16.8 %collective-permute-start.16 = (bf16[16,768]{1,0:T(8,128)(2,1)S(1)}, bf16[16,768]{1,0:T(8,128)(2,1)S(1)}, u32[]{:S(2)}, u32[]{:S(2)}) collective-permute-start(bf16[16,768]{1,0:T(8,128)(2,1)S(1)} %convert.130), channel_id=1, source_target_pairs={{0,4},{4,8},{8,12},{12,16},{16,20},{20,24},{24,28},{28,32},{32,36}... | collective-permute-start | bytes 73736
  513.1 15.4 %collective-permute-start.1 = (bf16[16,768]{1,0:T(8,128)(2,1)S(1)}, bf16[16,768]{1,0:T(8,128)(2,1)S(1)}, u32[]{:S(2)}, u32[]{:S(2)}) collective-permute-start(bf16[16,768]{1,0:T(8,128)(2,1)S(1)} %convert.131), channel_id=1, source_target_pairs={{0,8},{4,12},{8,16},{12,20},{16,24},{20,28},{24,32},{28,36},{32,40... | collective-permute-start | bytes 73736
  515.3 15.3 %collective-permute-start.2 = (bf16[16,768]{1,0:T(8,128)(2,1)S(1)}, bf16[16,768]{1,0:T(8,128)(2,1)S(1)}, u32[]{:S(2)}, u32[]{:S(2)}) collective-permute-start(bf16[16,768]{1,0:T(8,128)(2,1)S(1)} %convert.131), channel_id=1, source_target_pairs={{0,12},{4,16},{8,20},{12,24},{16,28},{20,32},{24,36},{28,40},{32,4... | collective-permute-start | bytes 73736
  517.6 14.6 %collective-permute-start.3 = (bf16[16,768]{1,0:T(8,128)(2,1)S(1)}, bf16[16,768]{1,0:T(8,128)(2,1)S(1)}, u32[]{:S(2)}, u32[]{:S(2)}) collective-permute-start(bf16[16,768]{1,0:T(8,128)(2,1)S(1)} %convert.131), channel_id=1, source_target_pairs={{0,16},{4,20},{8,24},{12,28},{16,32},{20,36},{24,40},{28,44},{32,4... | collective-permute-start | bytes 73736
  522.4 11.1 %collective-permute-start.4 = (bf16[16,768]{1,0:T(8,128)(2,1)S(1)}, bf16[16,768]{1,0:T(8,128)(2,1)S(1)}, u32[]{:S(2)}, u32[]{:S(2)}) collective-permute-start(bf16[16,768]{1,0:T(8,128)(2,1)S(1)} %convert.131), channel_id=1, source_target_pairs={{0,20},{4,24},{8,28},{12,32},{16,36},{20,40},{24,44},{28,48},{32,5... | collective-permute-start | bytes 73736
  527.0 8.2 %collective-permute-start.5 = (bf16[16,768]{1,0:T(8,128)(2,1)S(1)}, bf16[16,768]{1,0:T(8,128)(2,1)S(1)}, u32[]{:S(2)}, u32[]{:S(2)}) collective-permute-start(bf16[16,768]{1,0:T(8,128)(2,1)S(1)} %convert.131), channel_id=1, source_target_pairs={{0,24},{4,28},{8,32},{12,36},{16,40},{20,44},{24,48},{28,52},{32,5... | collective-permute-start | bytes 73736
  528.5 9.9 %collective-permute-start.6 = (bf16[16,768]{1,0:T(8,128)(2,1)S(1)}, bf16[16,768]{1,0:T(8,128)(2,1)S(1)}, u32[]{:S(2)}, u32[]{:S(2)}) collective-permute-start(bf16[16,768]{1,0:T(8,128)(2,1)S(1)} %convert.131), channel_id=1, source_target_pairs={{0,28},{4,32},{8,36},{12,40},{16,44},{20,48},{24,52},{28,56},{32,6... | collective-permute-start | bytes 73736
  530.6 9.8 %collective-permute-start.7 = (bf16[16,768]{1,0:T(8,128)(2,1)S(1)}, bf16[16,768]{1,0:T(8,128)(2,1)S(1)}, u32[]{:S(2)}, u32[]{:S(2)}) collective-permute-start(bf16[16,768]{1,0:T(8,128)(2,1)S(1)} %convert.131), channel_id=1, source_target_pairs={{0,32},{4,36},{8,40},{12,44},{16,48},{20,52},{24,56},{28,60},{32,6... | collective-permute-start | bytes 73736
  532.2 10.1 %collective-permute-start.8 = (bf16[16,768]{1,0:T(8,128)(2,1)S(1)}, bf16[16,768]{1,0:T(8,128)(2,1)S(1)}, u32[]{:S(2)}, u32[]{:S(2)}) collective-permute-start(bf16[16,768]{1,0:T(8,128)(2,1)S(1)} %convert.131), channel_id=1, source_target_pairs={{0,36},{4,40},{8,44},{12,48},{16,52},{20,56},{24,60},{28,64},{32,6... | collective-permute-start | bytes 73736
  533.5 10.7 %collective-permute-start.9 = (bf16[16,768]{1,0:T(8,128)(2,1)S(1)}, bf16[16,768]{1,0:T(8,128)(2,1)S(1)}, u32[]{:S(2)}, u32[]{:S(2)}) collective-permute-start(bf16[16,768]{1,0:T(8,128)(2,1)S(1)} %convert.131), channel_id=1, source_target_pairs={{0,40},{4,44},{8,48},{12,52},{16,56},{20,60},{24,64},{28,68},{32,7... | collective-permute-start | bytes 73736
  535.2 10.9 %collective-permute-start.10 = (bf16[16,768]{1,0:T(8,128)(2,1)S(1)}, bf16[16,768]{1,0:T(8,128)(2,1)S(1)}, u32[]{:S(2)}, u32[]{:S(2)}) collective-permute-start(bf16[16,768]{1,0:T(8,128)(2,1)S(1)} %convert.131), channel_id=1, source_target_pairs={{0,44},{4,48},{8,52},{12,56},{16,60},{20,64},{24,68},{28,72},{32,7... | collective-permute-start | bytes 73736
  538.4 19.2 %collective-permute-start.11 = (bf16[16,768]{1,0:T(8,128)(2,1)S(1)}, bf16[16,768]{1,0:T(8,128)(2,1)}, u32[]{:S(2)}, u32[]{:S(2)}) collective-permute-start(bf16[16,768]{1,0:T(8,128)(2,1)S(1)} %convert.131), channel_id=1, source_target_pairs={{0,48},{4,52},{8,56},{12,60},{16,64},{20,68},{24,72},{28,76},{32,8... | collective-permute-start | bytes 73736
  540.4 17.2 %collective-permute-start.12 = (bf16[16,768]{1,0:T(8,128)(2,1)S(1)}, bf16[16,768]{1,0:T(8,128)(2,1)}, u32[]{:S(2)}, u32[]{:S(2)}) collective-permute-start(bf16[16,768]{1,0:T(8,128)(2,1)S(1)} %convert.131), channel_id=1, source_target_pairs={{0,52},{4,56},{8,60},{12,64},{16,68},{20,72},{24,76},{28,80},{32,8... | collective-permute-start | bytes 73736
  542.3 15.3 %collective-permute-start.13 = (bf16[16,768]{1,0:T(8,128)(2,1)S(1)}, bf16[16,768]{1,0:T(8,128)(2,1)}, u32[]{:S(2)}, u32[]{:S(2)}) collective-permute-start(bf16[16,768]{1,0:T(8,128)(2,1)S(1)} %convert.131), channel_id=1, source_target_pairs={{0,56},{4,60},{8,64},{12,68},{16,72},{20,76},{24,80},{28,84},{32,8... | collective-permute-start | bytes 73736
  544.2 13.5 %collective-permute-start.14 = (bf16[16,768]{1,0:T(8,128)(2,1)S(1)}, bf16[16,768]{1,0:T(8,128)(2,1)}, u32[]{:S(2)}, u32[]{:S(2)}) collective-permute-start(bf16[16,768]{1,0:T(8,128)(2,1)S(1)} %convert.131), channel_id=1, source_target_pairs={{0,60},{4,64},{8,68},{12,72},{16,76},{20,80},{24,84},{28,88},{32,9... | collective-permute-start | bytes 73736
  546.1 11.6 %collective-permute-start = (bf16[16,768]{1,0:T(8,128)(2,1)S(1)}, bf16[16,768]{1,0:T(8,128)(2,1)}, u32[]{:S(2)}, u32[]{:S(2)}) collective-permute-start(bf16[16,768]{1,0:T(8,128)(2,1)S(1)} %convert.131), channel_id=1, source_target_pairs={{0,4},{4,8},{8,12},{12,16},{16,20},{20,24},{24,28},{28,32},{32,36}... | collective-permute-start | bytes 73736
  (61 other events, 1126.0 us)
Sparse Core Ops, SparseCore 0:
  568.2 35.7 all-reduce.12
where the time goes:
time: 684 us; the launch traced here: 672 us
  blocking collectives  249 us (36%)
  starting transfers between devices  185 us (27%)
  local copies, waits for them, and re-layouts  81.8 us (12%)
  other arithmetic  63.7 us (9%)
  waiting for transfers between devices  40 us (6%)
  matrix products  34.8 us (5%)
  between operations  17 us (2%)
    unnamed x1, blocking collectives  167 us
    unnamed x64, starting transfers between devices  149 us
    psum x1, blocking collectives, body(): vector_totals = lax.psum((vectors[0], vectors[1], vectors[2]), ('dp', 'mp'))  73.1 us
    dot_general x18, matrix products, mixing_weights(): return jnp.einsum(form, left, right, preferred_element_type=jnp.float32)  34.8 us
    unnamed x124, local copies, waits for them, and re-layouts  29.4 us
    all_to_all x1, waiting for transfers between devices, body(): lax.all_to_all(flat_found, 'dp', split_axis=0, concat_axis=0, tiled=True)  22.1 us
    another operation x3, other arithmetic  18.2 us
    all_to_all x1, starting transfers between devices, body(): lax.all_to_all(request, 'dp', split_axis=0, concat_axis=0, tiled=True)  14.3 us
  transfers between devices with their start and end apart: 70, of which 4 were waited for; matrix products, arithmetic and copies ran while one was open for 31% of the time, Pallas kernels for 0%

commit v1 on v0

v1 whole, which is shorter than its diff:
```python
import jax
import jax.numpy as jnp
from jax import lax
from jax.experimental import pallas as pl
from jax.experimental.pallas import tpu as pltpu
from jax.sharding import Mesh
from jax.sharding import PartitionSpec as P

HEADS = 12
LIST_LEN = 256
EPSILON = 1e-06
SCORE_CAP = 20.0
RANK_CAP = 30.0

ROWS = ("y", "z", "c")
CAP = 32
SLAB = 192
BF = jnp.bfloat16
F32 = jnp.float32
MIB = 1024 * 1024


def dot(a, b, ca=1, cb=0):
    return lax.dot_general(a, b, (((ca,), (cb,)), ((), ())), preferred_element_type=F32)


def iota(shape, dim):
    return lax.broadcasted_iota(jnp.int32, shape, dim)


def whole(n):
    return [pl.BlockSpec(memory_space=pltpu.VMEM)] * n


def call(kernel, out_shape, args, mib, flops, size, scratch=()):
    outs = out_shape if isinstance(out_shape, (list, tuple)) else [out_shape]
    specs = whole(len(outs))
    return pl.pallas_call(
        kernel,
        out_shape=out_shape,
        in_specs=whole(len(args)),
        out_specs=specs if isinstance(out_shape, (list, tuple)) else specs[0],
        scratch_shapes=list(scratch),
        compiler_params=pltpu.CompilerParams(vmem_limit_bytes=mib * MIB),
        cost_estimate=pl.CostEstimate(flops=flops, bytes_accessed=size, transcendentals=0),
    )(*args)


def low_half(shape):
    return iota(shape, len(shape) - 1) < 64


def swap_halves(t):
    return jnp.concatenate([t[..., 64:], t[..., :64]], axis=-1)


def spread_tail(t):
    t = t.astype(F32)
    other = swap_halves(t)
    low = low_half(t.shape)
    return jnp.concatenate([jnp.where(low, t, other), jnp.where(low, other, t)], axis=1)


def unpack(block):
    b, rows, _ = block.shape
    n = rows // 3
    main = block[:, : 2 * n, :].reshape(b * 2 * n, 128)
    tail = spread_tail(block[:, 2 * n :, :]).astype(BF).reshape(b * 2 * n, 128)
    return jnp.concatenate([main, tail], axis=1)


def pack(full, n):
    tail = full[:, 128:]
    tail = jnp.where(low_half((n, 128)), tail[:n], tail[n:])
    return jnp.concatenate([full[:, :128], tail], axis=0).astype(BF)


def as_column(row):
    return jnp.transpose(jnp.broadcast_to(row, (128, 128)))


def routing_kernel(ids_ref, place_ref, request_ref, slot_ref):
    place = place_ref[...]
    lists = place.shape[1]
    lane = iota((128, 128), 1)
    owner_of_list = jnp.broadcast_to(place >> 3, (128, lists))
    row = iota((128, lists), 0)
    lookup = jnp.where(owner_of_list == row, 1.0, 0.0)
    lookup = jnp.where(row == 64, jnp.broadcast_to(place & 7, (128, lists)).astype(F32), lookup)
    lookup = lookup.astype(BF)
    before = (iota((128, 128), 1) < iota((128, 128), 0)).astype(F32).astype(BF)
    carry = jnp.zeros((1, 128), F32)
    request = jnp.zeros((128, 128), F32)
    for q in range(ids_ref.shape[0]):
        ids = as_column(ids_ref[q : q + 1, :])
        list_id = ids >> 8
        chosen = jnp.concatenate(
            [(list_id == lane + 128 * t).astype(F32).astype(BF) for t in range(lists // 128)], axis=1
        )
        found = dot(chosen, lookup, 1, 1)
        sub = jnp.sum(jnp.where(lane == 64, found, 0.0), 1, keepdims=True)
        onehot = jnp.where(lane < 64, found, 0.0)
        onehot_low = onehot.astype(BF)
        ahead = dot(before, onehot_low) + carry
        carry = carry + jnp.sum(onehot, 0, keepdims=True)
        rank = jnp.sum(onehot * ahead, 1, keepdims=True)
        owner = jnp.sum(onehot * lane.astype(F32), 1, keepdims=True)
        slot = jnp.broadcast_to(owner * CAP + rank, (128, 128))
        slot_ref[q : q + 1, :] = jnp.transpose(slot)[0:1, :].astype(jnp.int32)
        rank = rank.astype(jnp.int32)
        place_in = (ids & 255).astype(F32)
        entry = jnp.where(rank == lane, sub + 1.0, jnp.where(rank == lane - CAP, place_in, 0.0))
        request = request + dot(onehot_low, entry.astype(BF), 0, 0)
    high = request[:64, :CAP]
    low = request[:64, CAP : 2 * CAP]
    asked = (high - 1.0) * LIST_LEN + low
    request_ref[...] = jnp.where(high > 0.5, asked, -1.0).astype(jnp.int32)


def owner_kernel(asked_ref, table_ref, out_ref):
    groups = asked_ref.shape[0]
    part = groups // 4
    asked = asked_ref[...]
    asked = jnp.concatenate([asked[part * k : part * (k + 1)] for k in range(4)], axis=1)
    table = table_ref[...]
    stored = table.shape[0]
    tail = table[:, 128:].astype(F32)
    table = jnp.concatenate([table[:, :128], jnp.concatenate([tail, tail], 1).astype(BF)], axis=1)
    step = 4
    for r in range(0, part, step):
        column = jnp.concatenate([as_column(asked[r + i : r + i + 1]) for i in range(step)], axis=0)
        lane = iota((128 * step, 128), 1)
        chosen = jnp.concatenate(
            [(column == lane + 128 * t).astype(F32).astype(BF) for t in range(stored // 128)], axis=1
        )
        rows = dot(chosen, table)
        for i in range(step):
            for k in range(4):
                at = 128 * i + CAP * k
                out_ref[part * k + r + i] = pack(rows[at : at + CAP], CAP // 2)


def pieces_kernel(slot_ref, fetched_ref, out_ref):
    fetched = unpack(fetched_ref[...])
    slots = fetched.shape[0]
    for m in range(out_ref.shape[0]):
        column = jnp.concatenate([as_column(slot_ref[2 * m + i : 2 * m + i + 1, :]) for i in (0, 1)], axis=0)
        lane = iota((256, 128), 1)
        chosen = jnp.concatenate(
            [(column == lane + 128 * t).astype(F32).astype(BF) for t in range(slots // 128)], axis=1
        )
        out_ref[m] = pack(dot(chosen, fetched), 128)


def slots_kernel(slot_ref, grads_ref, out_ref):
    grads = unpack(grads_ref[...])
    groups = out_ref.shape[0]
    step = 16 * CAP
    for r in range(0, groups * CAP, step):
        row = iota((step, 128), 0) + r
        chosen = jnp.concatenate(
            [
                (jnp.broadcast_to(slot_ref[q : q + 1, :], (step, 128)) == row).astype(F32).astype(BF)
                for q in range(slot_ref.shape[0])
            ],
            axis=1,
        )
        rows = dot(chosen, grads)
        for i in range(16):
            out_ref[r // CAP + i] = pack(rows[CAP * i : CAP * (i + 1)], CAP // 2)


def landing_kernel(asked_ref, arrived_ref, out_ref):
    arrived = unpack(arrived_ref[...])
    stored = out_ref.shape[0]
    step = 512
    for r in range(0, stored, step):
        row = iota((step, 128), 0) + r
        chosen = jnp.concatenate(
            [
                (jnp.broadcast_to(asked_ref[q : q + 1, :], (step, 128)) == row).astype(F32).astype(BF)
                for q in range(asked_ref.shape[0])
            ],
            axis=1,
        )
        out_ref[r : r + step, :] = dot(chosen, arrived)[:, :SLAB]


def lane_mean(x):
    return jnp.sum(x, 1, keepdims=True) * (1.0 / x.shape[1])


def step_kernel(
    core_ref,
    rows_ref,
    query_ref,
    labels_ref,
    wq_ref,
    wk_ref,
    wv_ref,
    wo_ref,
    gain_attn_ref,
    gain_score_ref,
    w_score_ref,
    losses_ref,
    base_ref,
    query_grad_ref,
    keep_ref,
    send_ref,
    scores_t,
    attend_t,
    grads,
):
    queries, width = query_ref.shape
    size = 128
    head = width // HEADS
    pairs = HEADS // 2
    shrink = head ** (-0.5)
    low = low_half((size, 128))

    parts = []
    for m in range(rows_ref.shape[0]):
        main = rows_ref[m, :256, :].astype(F32)
        tail = rows_ref[m, 256:, :].astype(F32)
        parts += [main, jnp.concatenate([tail[:, :64], tail[:, 64:]], axis=0)]
    rows_in = jnp.concatenate(parts, axis=1)
    vecs = query_ref[...].astype(F32)
    vecs = jnp.concatenate([jnp.broadcast_to(vecs[q : q + 1], (size, width)) for q in range(queries)], axis=0)
    base = rows_in + vecs
    inv_one = 1.0 / jnp.sqrt(lane_mean(base * base) + EPSILON)
    normed_one = base * inv_one
    gain_attn = gain_attn_ref[...]
    first_input = (normed_one * gain_attn).astype(BF)
    q_all = dot(first_input, wq_ref[...]).astype(BF)
    k_all = dot(first_input, wk_ref[...]).astype(BF)
    v_all = dot(first_input, wv_ref[...]).astype(BF)

    def cut(x, q, p):
        return x[size * q : size * (q + 1), 128 * p : 128 * (p + 1)]

    zero = jnp.zeros((size, 128), BF)

    def heads_apart(x):
        return jnp.concatenate([jnp.where(low, x, zero), jnp.where(low, zero, x)], axis=0)

    def heads_joined(x):
        return jnp.where(low, x[:size], x[size:])

    context = []
    for q in range(queries):
        line = []
        for p in range(pairs):
            logits = dot(cut(k_all, q, p), heads_apart(cut(q_all, q, p)), 1, 1)
            th = jnp.tanh(logits * (shrink / SCORE_CAP))
            raised = jnp.exp(SCORE_CAP * th)
            attend = raised * (1.0 / jnp.sum(raised, 0, keepdims=True))
            scores_t[q * pairs + p] = th
            attend_t[q * pairs + p] = attend
            line.append(heads_joined(dot(attend.astype(BF), cut(v_all, q, p), 0, 0)))
        context.append(jnp.concatenate(line, axis=1))
    context = jnp.concatenate(context, axis=0).astype(BF)

    mixed = base + dot(context, wo_ref[...])
    inv_two = 1.0 / jnp.sqrt(lane_mean(mixed * mixed) + EPSILON)
    normed_two = mixed * inv_two
    gain_score = gain_score_ref[...]
    w_score = w_score_ref[...]
    scaled_two = normed_two * gain_score
    capped_scores = jnp.tanh(jnp.sum(scaled_two * w_score, 1, keepdims=True) * (1.0 / RANK_CAP))
    scores = RANK_CAP * capped_scores
    raised = jnp.exp(scores)
    relevance = jnp.exp(labels_ref[...].astype(F32))
    target = relevance / jnp.sum(relevance, 1, keepdims=True)
    diffs = []
    for q in range(queries):
        at = slice(size * q, size * (q + 1))
        total = jnp.sum(raised[at], 0, keepdims=True)
        wanted = as_column(target[q : q + 1])[:, 0:1]
        loss = jnp.log(total) - jnp.sum(wanted * scores[at], 0, keepdims=True)
        losses_ref[q : q + 1, :] = jnp.broadcast_to(loss, (1, 128))
        diffs.append(raised[at] / total - wanted)
    diff_raw = jnp.concatenate(diffs, axis=0) * (1.0 - capped_scores * capped_scores)
    grad_w_score = jnp.sum(scaled_two * diff_raw, 0, keepdims=True)
    diff_scaled = diff_raw * w_score
    grad_gain_score = jnp.sum(normed_two * diff_scaled, 0, keepdims=True)
    diff_normed = diff_scaled * gain_score
    diff_mixed = (diff_normed - normed_two * lane_mean(diff_normed * normed_two)) * inv_two
    diff_low = diff_mixed.astype(BF)
    diff_context = dot(diff_low, wo_ref[...], 1, 1).astype(BF)

    diff_q, diff_k, diff_v = [], [], []
    for q in range(queries):
        line_q, line_k, line_v = [], [], []
        for p in range(pairs):
            th = scores_t[q * pairs + p]
            attend = attend_t[q * pairs + p]
            split = heads_apart(cut(diff_context, q, p))
            diff_attend = dot(cut(v_all, q, p), split, 1, 1)
            line_v.append(dot(attend.astype(BF), split))
            inner = diff_attend - jnp.sum(attend * diff_attend, 0, keepdims=True)
            diff_logits = (attend * inner * (1.0 - th * th) * shrink).astype(BF)
            line_q.append(heads_joined(dot(diff_logits, cut(k_all, q, p), 0, 0)))
            line_k.append(dot(diff_logits, heads_apart(cut(q_all, q, p))))
        diff_q.append(jnp.concatenate(line_q, axis=1))
        diff_k.append(jnp.concatenate(line_k, axis=1))
        diff_v.append(jnp.concatenate(line_v, axis=1))
    diff_q = jnp.concatenate(diff_q, axis=0).astype(BF)
    diff_k = jnp.concatenate(diff_k, axis=0).astype(BF)
    diff_v = jnp.concatenate(diff_v, axis=0).astype(BF)

    diff_input = dot(diff_q, wq_ref[...], 1, 1) + dot(diff_k, wk_ref[...], 1, 1) + dot(diff_v, wv_ref[...], 1, 1)
    grad_gain_attn = jnp.sum(normed_one * diff_input, 0, keepdims=True)
    diff_first = diff_input * gain_attn
    diff_base = diff_mixed + (diff_first - normed_one * lane_mean(diff_first * normed_one)) * inv_one
    for q in range(queries):
        query_grad_ref[q : q + 1, :] = jnp.sum(diff_base[size * q : size * (q + 1)], 0, keepdims=True)
    for m in range(base_ref.shape[0]):
        slab = diff_base[:, SLAB * m : SLAB * (m + 1)]
        base_ref[m, :256, :] = slab[:, :128].astype(BF)
        base_ref[m, 256:, :] = jnp.concatenate([slab[:128, 128:], slab[128:, 128:]], axis=1).astype(BF)

    grads[0] = dot(first_input, diff_q, 0, 0)
    grads[1] = dot(first_input, diff_k, 0, 0)
    grads[2] = dot(first_input, diff_v, 0, 0)
    grads[3] = dot(context, diff_low, 0, 0)
    vectors = [
        v[:, 128 * t : 128 * (t + 1)]
        for v in (grad_gain_attn, grad_gain_score, grad_w_score)
        for t in range(width // 128)
    ]
    vectors = jnp.concatenate(vectors + [jnp.zeros((32 - len(vectors), 128), F32)], axis=0)
    first_core = core_ref[0] == 0

    def assemble(at, carry):
        chunk = [grads[i, pl.ds(pl.multiple_of(24 * at, 8), 24), :] for i in range(4)]
        halves = [jnp.concatenate([g[12 * c : 12 * (c + 1)] for g in chunk], axis=0) for c in (0, 1)]
        for m in range(4):
            blocks = []
            for rows48 in halves:
                tiles = []
                for h in range(9 * m, 9 * m + 9):
                    rb, t = h // 6, h % 6
                    tiles.append(rows48[8 * rb : 8 * rb + 8, 128 * t : 128 * (t + 1)])
                blocks.append(jnp.concatenate(tiles + [vectors[8 * m : 8 * m + 8]], axis=0).astype(BF))
            keep_ref[m, at] = jnp.where(first_core, blocks[0], blocks[1])
            send_ref[m, at] = jnp.where(first_core, blocks[1], blocks[0])
        return carry

    lax.fori_loop(0, keep_ref.shape[1], assemble, 0)


def finish_kernel(blocks_ref, q_ref, k_ref, v_ref, o_ref, vec_ref):
    blocks = blocks_ref[...].astype(F32)
    tiles = [blocks[m, 8 * i : 8 * i + 8] for m in range(4) for i in range(9)]
    rows48 = jnp.concatenate([jnp.concatenate(tiles[6 * rb : 6 * rb + 6], axis=1) for rb in range(6)], axis=0)
    for i, ref in enumerate((q_ref, k_ref, v_ref, o_ref)):
        ref[...] = rows48[12 * i : 12 * (i + 1)]
    vec_ref[...] = jnp.concatenate([blocks[m, 72:] for m in range(4)], axis=0)


def shape(dims, kind=BF):
    return jax.ShapeDtypeStruct(dims, kind)


def swap(x, axes):
    return lax.all_to_all(x, axes, split_axis=0, concat_axis=0, tiled=True)


def body(
    cand_item,
    list_place,
    item_table,
    query_vec,
    labels,
    query_weight,
    key_weight,
    value_weight,
    output_weight,
    gain_attn,
    gain_score,
    w_score,
):
    queries, size = cand_item.shape
    stored, slab = item_table.shape
    width = query_vec.shape[1]
    n_dp = lax.axis_size(ROWS)
    n_mp = lax.axis_size("x")
    n_yz = lax.axis_size(("y", "z"))
    slots = n_dp * CAP

    ids = lax.all_gather(cand_item, "x", axis=0, tiled=True)
    request, slot = call(
        routing_kernel,
        [shape((n_dp, CAP), jnp.int32), shape((n_mp * queries, size), jnp.int32)],
        (ids, list_place.reshape(1, -1)),
        24, 3 * 10**8, 10**6,
    )
    asked = swap(request, ROWS)
    found = call(
        owner_kernel, shape((n_dp, 48, 128)), (asked, item_table), 40, 2 * 10**9, 2 * 10**6
    )
    fetched = swap(found, ROWS)
    pieces = call(pieces_kernel, shape((n_mp, 384, 128)), (slot, fetched), 40, 10**9, 2 * 10**6)
    rows_in = swap(pieces, "x")
    core = lax.axis_index("c").astype(jnp.int32).reshape(1)
    args = (
        core, rows_in, query_vec, labels,
        query_weight, key_weight, value_weight, output_weight,
        gain_attn.reshape(1, -1), gain_score.reshape(1, -1), w_score.reshape(1, -1),
    )
    outs = [
        shape((queries, 128), F32),
        shape((n_mp, 384, 128)),
        shape((queries, width), F32),
        shape((n_mp, n_yz, 80, 128)),
        shape((n_mp, n_yz, 80, 128)),
    ]
    losses, diff_base, query_grad, keep, send = pl.pallas_call(
        step_kernel,
        out_shape=outs,
        in_specs=[pl.BlockSpec(memory_space=pltpu.SMEM)] + whole(len(args) - 1),
        out_specs=whole(len(outs)),
        scratch_shapes=[
            pltpu.VMEM((HEADS * queries // 2, 128, 256), F32),
            pltpu.VMEM((HEADS * queries // 2, 128, 256), F32),
            pltpu.VMEM((4, width, width), F32),
        ],
        compiler_params=pltpu.CompilerParams(vmem_limit_bytes=56 * MIB),
        cost_estimate=pl.CostEstimate(flops=5 * 10**9, bytes_accessed=12 * 10**6, transcendentals=0),
    )(*args)

    column_grads = swap(diff_base, "x")
    outgoing = call(
        slots_kernel, shape((n_dp, 48, 128)), (slot, column_grads), 40, 10**9, 2 * 10**6
    )
    arrived = swap(outgoing, ROWS)
    table_grad = call(
        landing_kernel,
        shape((stored, slab), F32),
        (asked.reshape(slots // 128, 128), arrived),
        40, 2 * 10**9, 4 * 10**6,
    )

    other = lax.ppermute(send, "c", [(0, 1), (1, 0)])
    both = (keep.astype(F32) + other.astype(F32)).astype(BF)

    def summed(x):
        return jnp.sum(x.astype(F32), 0).astype(BF)

    over_x = summed(swap(both, "x"))
    over_all = summed(swap(over_x, ("y", "z")))
    blocks = lax.all_gather(over_all, "x", axis=0, tiled=False)
    rows = width // n_dp
    finished = call(
        finish_kernel,
        [shape((rows, width), F32)] * 4 + [shape((32, 128), F32)],
        (blocks,), 8, 10**6, 10**6,
    )
    vectors = finished[4].reshape(-1)
    return (
        losses[:, 0],
        table_grad,
        query_grad,
        finished[0],
        finished[1],
        finished[2],
        finished[3],
        vectors[:width],
        vectors[width : 2 * width],
        vectors[2 * width : 3 * width],
    )


def solution(mesh):
    grid = Mesh(mesh.devices.reshape(4, 8, 2, 4), ("y", "z", "c", "x"))
    each = P(("y", "z", "c", "x"), None)
    placed = (each, P(), P(ROWS, "x"), each, each, P(), P(), P(), P(), P(), P(), P())
    return jax.shard_map(
        body,
        mesh=grid,
        in_specs=placed,
        out_specs=(
            P(("y", "z", "c", "x")),
            P(ROWS, "x"),
            each,
            P(ROWS, None),
            P(ROWS, None),
            P(ROWS, None),
            P(ROWS, None),
            P(),
            P(),
            P(),
        ),
        check_vma=False,
    )
```

time: 684 us -> 215 us (0.31)
  the two profiles are of different devices: /device:TPU:1 before, /device:TPU:32 now
where the time goes in v1:
time: 215 us; the launch traced here: 214 us
  waiting for transfers between devices  82 us (38%)
  blocking collectives  49.3 us (23%)
  starting transfers between devices  36.4 us (17%)
  Pallas kernels  28.8 us (13%)
  other arithmetic  8.98 us (4%)
  local copies, waits for them, and re-layouts  8.13 us (4%)
    all_to_all x6, waiting for transfers between devices, swap(): return lax.all_to_all(x, axes, split_axis=0, concat_axis=0, tiled=True)  80.4 us
    all_to_all x6, starting transfers between devices, swap(): return lax.all_to_all(x, axes, split_axis=0, concat_axis=0, tiled=True)  36.4 us
    all_to_all x1, blocking collectives, swap(): return lax.all_to_all(x, axes, split_axis=0, concat_axis=0, tiled=True)  27.4 us
    pallas_call x1, Pallas kernels, body(): pl.pallas_call(step_kernel, out_shape=outs, in_specs=[pl.BlockSpec(memory...  15.5 us
    pallas_call x6, Pallas kernels, call(): pl.pallas_call(kernel, out_shape=out_shape, in_specs=whole(len(args)), ou...  13.3 us
    all_gather x1, blocking collectives, body(): blocks = lax.all_gather(over_all, 'x', axis=0, tiled=False)  11.9 us
    all_gather x1, blocking collectives, body(): ids = lax.all_gather(cand_item, 'x', axis=0, tiled=True)  9.97 us
    unnamed x14, local copies, waits for them, and re-layouts  4.57 us
  transfers between devices with their start and end apart: 7, of which 7 were waited for; matrix products, arithmetic and copies ran while one was open for 6% of the time, Pallas kernels for 2%

profile of v1, /device:TPU:32, one launch (start us, length us, event | category | flops | bytes accessed | tf_op | source)
XLA Modules:
  0.0 214.5 jit_solution(12811128019742759920)
XLA Ops:
  0.6 10.0 %all-gather.1 = s32[4,2,128]{2,1,0:T(2,128)S(1)} all-gather(s32[1,2,128]{2,1,0:T(2,128)} %bitcast.19), channel_id=1, replica_groups=mesh['y'=4,'z'=8,'c'=2,'x'=4] {'x'}, dimensions={0}, use_global_device_ids=true | all-gather | bytes 5120 | tf_op jit(solution)/shard_map/all_gather | solution.py:391
  10.6 0.0 copy-start
  10.6 0.7 copy-done
  11.3 3.4 %shard_map.195 = (s32[64,32]{1,0:T(8,128)}, s32[8,128]{1,0:T(8,128)S(1)}) custom-call(s32[8,128]{1,0:T(8,128)S(1)} %bitcast.17, s32[1,512]{1,0:T(1,128)S(1)} %bitcast.18), custom_call_target="tpu_custom_call" | custom-call | flops 300000000 | bytes 1000000 | tf_op jit(solution)/shard_map/pallas_call | solution.py:38
  14.7 11.8 %all-to-all-start = ((s32[64,1,32]{2,1,0:T(1,128)}), s32[64,1,32]{2,1,0:T(1,128)S(1)}, u32[]{:S(2)}, u32[]{:S(2)}) async-start(s32[64,1,32]{2,1,0:T(1,128)} %bitcast.5), calls=%async_computation | async-start | bytes 65536 | tf_op jit(solution)/shard_map/all_to_all | solution.py:366
  26.5 1.4 copy.30.table_ref
  27.9 7.0 %all-to-all-done = s32[64,1,32]{2,1,0:T(1,128)S(1)} async-done(((s32[64,1,32]{2,1,0:T(1,128)}), s32[64,1,32]{2,1,0:T(1,128)S(1)}, u32[]{:S(2)}, u32[]{:S(2)}) %all-to-all-start) | async-done | bytes 8224 | tf_op jit(solution)/shard_map/all_to_all | solution.py:366
  35.0 2.5 %shard_map.196 = bf16[64,48,128]{2,1,0:T(8,128)(2,1)S(1)} custom-call(s32[64,32]{1,0:T(8,128)S(1)} %bitcast.16, bf16[2048,192]{1,0:T(8,128)(2,1)S(1)} %copy.30.table_ref), custom_call_target="tpu_custom_call" | custom-call | flops 2000000000 | bytes 2000000 | tf_op jit(solution)/shard_map/pallas_call | solution.py:38
  37.5 27.4 %all_to_all.41.fetched_ref = bf16[64,48,128]{2,1,0:T(8,128)(2,1)S(1)} all-to-all(bf16[64,48,128]{2,1,0:T(8,128)(2,1)S(1)} %shard_map.196), channel_id=1, replica_groups=mesh['y'=4,'z'=8,'c'=2,'x'=4] {'y','z','c'}, dimensions={0} | all-to-all | bytes 1572864 | tf_op jit(solution)/shard_map/all_to_all | solution.py:366
  64.9 0.0 copy-start.2
  64.9 0.0 copy-start.3
  64.9 0.0 copy-start.4
  64.9 2.1 shard_map.197
  67.0 3.6 %all-to-all-start.2 = ((bf16[4,384,128]{2,1,0:T(8,128)(2,1)}), bf16[4,384,128]{2,1,0:T(8,128)(2,1)S(1)}, u32[]{:S(2)}, u32[]{:S(2)}) async-start(bf16[4,384,128]{2,1,0:T(8,128)(2,1)} %shard_map.197), calls=%async_computation.2 | async-start | bytes 786432 | tf_op jit(solution)/shard_map/all_to_all | solution.py:366
  70.7 0.0 copy-done.2
  70.7 0.6 reshape.47.gain_attn_ref
  71.3 0.0 copy-done.3
  71.3 0.6 reshape.48.gain_score_ref
  71.9 0.0 copy-done.4
  71.9 0.6 reshape.49.w_score_ref
  72.4 6.1 %all-to-all-done.2.rows_ref = bf16[4,384,128]{2,1,0:T(8,128)(2,1)S(1)} async-done(((bf16[4,384,128]{2,1,0:T(8,128)(2,1)}), bf16[4,384,128]{2,1,0:T(8,128)(2,1)S(1)}, u32[]{:S(2)}, u32[]{:S(2)}) %all-to-all-start.2) | async-done | bytes 393248 | tf_op jit(solution)/shard_map/all_to_all | solution.py:366
  78.6 0.0 copy-start.1
  78.6 0.7 copy-done.1
  79.3 15.5 %shard_map.198 = (f32[2,128]{1,0:T(2,128)}, bf16[4,384,128]{2,1,0:T(8,128)(2,1)}, f32[2,768]{1,0:T(2,128)}, bf16[4,32,80,128]{3,2,1,0:T(8,128)(2,1)}, bf16[4,32,80,128]{3,2,1,0:T(8,128)(2,1)}) custom-call(s32[1]{0:T(128)} %bitcast.core_ref, bf16[4,384,128]{2,1,0:T(8,128)(2,1)} %copy-done.1, bf16[2,768]{1,0:T(2,128)(2,1)} %query_ref.1, s32[2,128]{1,0:T(2,128)} %labels_ref.1, ...), custom_call_target="tpu_custom_call" | custom-call | flops 5000000000 | bytes 12000000 | tf_op jit(solution)/shard_map/pallas_call | solution.py:418
  94.8 0.0 collective-permute-start
  94.8 3.5 %all-to-all-start.3 = ((bf16[4,384,128]{2,1,0:T(8,128)(2,1)}), bf16[4,384,128]{2,1,0:T(8,128)(2,1)S(1)}, u32[]{:S(2)}, u32[]{:S(2)}) async-start(bf16[4,384,128]{2,1,0:T(8,128)(2,1)} %get-tuple-element.25), calls=%async_computation.3 | async-start | bytes 786432 | tf_op jit(solution)/shard_map/all_to_all | solution.py:366
  98.3 1.7 collective-permute-done
  99.9 3.9 %add_convert_fusion = bf16[4,32,80,128]{3,2,1,0:T(8,128)(2,1)} fusion(bf16[4,32,80,128]{3,2,1,0:T(8,128)(2,1)S(1)} %collective-permute-done, bf16[4,32,80,128]{3,2,1,0:T(8,128)(2,1)} %get-tuple-element.27), kind=kLoop, calls=%fused_computation | loop fusion | flops 5242880 | bytes 7864320 | tf_op jit(solution)/shard_map/convert_element_type | solution.py:445
  103.9 3.4 %all-to-all-done.3.grads_ref = bf16[4,384,128]{2,1,0:T(8,128)(2,1)S(1)} async-done(((bf16[4,384,128]{2,1,0:T(8,128)(2,1)}), bf16[4,384,128]{2,1,0:T(8,128)(2,1)S(1)}, u32[]{:S(2)}, u32[]{:S(2)}) %all-to-all-start.3) | async-done | bytes 393248 | tf_op jit(solution)/shard_map/all_to_all | solution.py:366
  107.3 4.5 %all-to-all-start.5 = ((bf16[4,32,80,128]{3,2,1,0:T(8,128)(2,1)}), bf16[4,32,80,128]{3,2,1,0:T(8,128)(2,1)}, u32[]{:S(2)}, u32[]{:S(2)}) async-start(bf16[4,32,80,128]{3,2,1,0:T(8,128)(2,1)} %add_convert_fusion), calls=%async_computation.5 | async-start | bytes 5242880 | tf_op jit(solution)/shard_map/all_to_all | solution.py:366
  111.8 2.2 %shard_map.199 = bf16[64,48,128]{2,1,0:T(8,128)(2,1)} custom-call(s32[8,128]{1,0:T(8,128)S(1)} %get-tuple-element.22.slot_ref, bf16[4,384,128]{2,1,0:T(8,128)(2,1)S(1)} %all-to-all-done.3.grads_ref), custom_call_target="tpu_custom_call" | custom-call | flops 1000000000 | bytes 2000000 | tf_op jit(solution)/shard_map/pallas_call | solution.py:38
  114.0 30.0 %all-to-all-done.5 = bf16[4,32,80,128]{3,2,1,0:T(8,128)(2,1)} async-done(((bf16[4,32,80,128]{3,2,1,0:T(8,128)(2,1)}), bf16[4,32,80,128]{3,2,1,0:T(8,128)(2,1)}, u32[]{:S(2)}, u32[]{:S(2)}) %all-to-all-start.5) | async-done | bytes 2621472 | tf_op jit(solution)/shard_map/all_to_all | solution.py:366
  144.0 6.9 %all-to-all-start.4 = ((bf16[64,48,128]{2,1,0:T(8,128)(2,1)}), bf16[64,48,128]{2,1,0:T(8,128)(2,1)S(1)}, u32[]{:S(2)}, u32[]{:S(2)}) async-start(bf16[64,48,128]{2,1,0:T(8,128)(2,1)} %shard_map.199), calls=%async_computation.4 | async-start | bytes 1572864 | tf_op jit(solution)/shard_map/all_to_all | solution.py:366
  150.9 0.0 copy-start.5
  150.9 3.1 %reduce_sum.24 = bf16[32,80,128]{2,1,0:T(8,128)(2,1)} reduce(bf16[4,32,80,128]{3,2,1,0:T(8,128)(2,1)} %all-to-all-done.5, bf16[]{:T(256)} %constant.9.clone.1), dimensions={0}, to_apply=%region_0.0 | reduce | flops 983040 | bytes 3276802 | tf_op jit(solution)/shard_map/reduce_sum | solution.py:448
  154.0 19.5 %all-to-all-done.4.arrived_ref = bf16[64,48,128]{2,1,0:T(8,128)(2,1)S(1)} async-done(((bf16[64,48,128]{2,1,0:T(8,128)(2,1)}), bf16[64,48,128]{2,1,0:T(8,128)(2,1)S(1)}, u32[]{:S(2)}, u32[]{:S(2)}) %all-to-all-start.4) | async-done | bytes 786464 | tf_op jit(solution)/shard_map/all_to_all | solution.py:366
  173.5 6.2 %all-to-all-start.6 = ((bf16[32,80,128]{2,1,0:T(8,128)(2,1)}), bf16[32,80,128]{2,1,0:T(8,128)(2,1)}, u32[]{:S(2)}, u32[]{:S(2)}) async-start(bf16[32,80,128]{2,1,0:T(8,128)(2,1)} %reduce_sum.24), calls=%async_computation.6 | async-start | bytes 1310720 | tf_op jit(solution)/shard_map/all_to_all | solution.py:366
  179.7 0.5 broadcast.4
  180.2 0.7 reduce.7
  180.9 0.1 reshape.50.asked_ref
  181.0 0.0 copy-done.5
  181.0 0.6 slice_reduce_fusion
  181.6 2.4 %shard_map.200 = f32[2048,192]{1,0:T(8,128)S(1)} custom-call(s32[16,128]{1,0:T(8,128)S(1)} %reshape.50.asked_ref, bf16[64,48,128]{2,1,0:T(8,128)(2,1)S(1)} %all-to-all-done.4.arrived_ref), custom_call_target="tpu_custom_call" | custom-call | flops 2000000000 | bytes 4000000 | tf_op jit(solution)/shard_map/pallas_call | solution.py:38
  184.0 1.7 copy.31
  185.7 14.3 %all-to-all-done.6 = bf16[32,80,128]{2,1,0:T(8,128)(2,1)} async-done(((bf16[32,80,128]{2,1,0:T(8,128)(2,1)}), bf16[32,80,128]{2,1,0:T(8,128)(2,1)}, u32[]{:S(2)}, u32[]{:S(2)}) %all-to-all-start.6) | async-done | bytes 655392 | tf_op jit(solution)/shard_map/all_to_all | solution.py:366
  200.1 1.2 reduce_sum.25
  201.3 11.9 %all-gather = bf16[320,128]{1,0:T(8,128)(2,1)S(1)} all-gather(bf16[80,128]{1,0:T(8,128)(2,1)S(1)} %reduce_sum.25), channel_id=2, replica_groups=mesh['y'=4,'z'=8,'c'=2,'x'=4] {'x'}, dimensions={0}, use_global_device_ids=true | all-gather | bytes 102400 | tf_op jit(solution)/shard_map/all_gather | solution.py:452
  213.2 0.7 shard_map.201
  213.8 0.6 slice_bitcast_fusion
Async XLA Ops:
  10.6 0.7 copy-start
  14.7 20.2 %all-to-all-start = ((s32[64,1,32]{2,1,0:T(1,128)}), s32[64,1,32]{2,1,0:T(1,128)S(1)}, u32[]{:S(2)}, u32[]{:S(2)}) async-start(s32[64,1,32]{2,1,0:T(1,128)} %bitcast.5), calls=%async_computation | async-start | bytes 65536 | tf_op jit(solution)/shard_map/all_to_all | solution.py:366
  64.9 5.8 %copy-start.2 = (f32[768]{0:T(1024)S(1)}, f32[768]{0:T(1024)}, u32[]{:S(2)}) copy-start(f32[768]{0:T(1024)} %param.21) | copy-start | bytes 9220
  64.9 6.4 %copy-start.3 = (f32[768]{0:T(1024)S(1)}, f32[768]{0:T(1024)}, u32[]{:S(2)}) copy-start(f32[768]{0:T(1024)} %param.22) | copy-start | bytes 9220
  64.9 6.9 %copy-start.4 = (f32[768]{0:T(1024)S(1)}, f32[768]{0:T(1024)}, u32[]{:S(2)}) copy-start(f32[768]{0:T(1024)} %param.23) | copy-start | bytes 9220
  67.0 11.5 %all-to-all-start.2 = ((bf16[4,384,128]{2,1,0:T(8,128)(2,1)}), bf16[4,384,128]{2,1,0:T(8,128)(2,1)S(1)}, u32[]{:S(2)}, u32[]{:S(2)}) async-start(bf16[4,384,128]{2,1,0:T(8,128)(2,1)} %shard_map.197), calls=%async_computation.2 | async-start | bytes 786432 | tf_op jit(solution)/shard_map/all_to_all | solution.py:366
  78.6 0.7 copy-start.1
  94.8 5.1 %collective-permute-start = (bf16[4,32,80,128]{3,2,1,0:T(8,128)(2,1)}, bf16[4,32,80,128]{3,2,1,0:T(8,128)(2,1)S(1)}, u32[]{:S(2)}, u32[]{:S(2)}) collective-permute-start(bf16[4,32,80,128]{3,2,1,0:T(8,128)(2,1)} %get-tuple-element.28), channel_id=1, source_target_pairs={{0,4},{4,0},{1,5},{5,1},{2,6},{6,2},{3,7},{7,3},{8,12},{12,8},{9,1... | collective-permute-start | bytes 7864328 | tf_op jit(solution)/shard_map/ppermute | solution.py:444
  94.8 12.5 %all-to-all-start.3 = ((bf16[4,384,128]{2,1,0:T(8,128)(2,1)}), bf16[4,384,128]{2,1,0:T(8,128)(2,1)S(1)}, u32[]{:S(2)}, u32[]{:S(2)}) async-start(bf16[4,384,128]{2,1,0:T(8,128)(2,1)} %get-tuple-element.25), calls=%async_computation.3 | async-start | bytes 786432 | tf_op jit(solution)/shard_map/all_to_all | solution.py:366
  107.3 36.7 %all-to-all-start.5 = ((bf16[4,32,80,128]{3,2,1,0:T(8,128)(2,1)}), bf16[4,32,80,128]{3,2,1,0:T(8,128)(2,1)}, u32[]{:S(2)}, u32[]{:S(2)}) async-start(bf16[4,32,80,128]{3,2,1,0:T(8,128)(2,1)} %add_convert_fusion), calls=%async_computation.5 | async-start | bytes 5242880 | tf_op jit(solution)/shard_map/all_to_all | solution.py:366
  144.0 29.5 %all-to-all-start.4 = ((bf16[64,48,128]{2,1,0:T(8,128)(2,1)}), bf16[64,48,128]{2,1,0:T(8,128)(2,1)S(1)}, u32[]{:S(2)}, u32[]{:S(2)}) async-start(bf16[64,48,128]{2,1,0:T(8,128)(2,1)} %shard_map.199), calls=%async_computation.4 | async-start | bytes 1572864 | tf_op jit(solution)/shard_map/all_to_all | solution.py:366
  150.9 30.1 %copy-start.5 = (f32[2,128]{1,0:T(2,128)S(1)}, f32[2,128]{1,0:T(2,128)}, u32[]{:S(2)}) copy-start(f32[2,128]{1,0:T(2,128)} %get-tuple-element.24) | copy-start | bytes 3076
  173.5 26.6 %all-to-all-start.6 = ((bf16[32,80,128]{2,1,0:T(8,128)(2,1)}), bf16[32,80,128]{2,1,0:T(8,128)(2,1)}, u32[]{:S(2)}, u32[]{:S(2)}) async-start(bf16[32,80,128]{2,1,0:T(8,128)(2,1)} %reduce_sum.24), calls=%async_computation.6 | async-start | bytes 1310720 | tf_op jit(solution)/shard_map/all_to_all | solution.py:366

commit v2 on v1

--- a/solution.py
+++ b/solution.py
@@ -32,18 +32,34 @@
     return [pl.BlockSpec(memory_space=pltpu.VMEM)] * n
 
 
-def call(kernel, out_shape, args, mib, flops, size, scratch=()):
+def call(kernel, out_shape, args, mib, flops, size, scratch=(), scalar=False):
     outs = out_shape if isinstance(out_shape, (list, tuple)) else [out_shape]
     specs = whole(len(outs))
+    in_specs = whole(len(args))
+    if scalar:
+        in_specs[0] = pl.BlockSpec(memory_space=pltpu.SMEM)
     return pl.pallas_call(
         kernel,
         out_shape=out_shape,
-        in_specs=whole(len(args)),
+        in_specs=in_specs,
         out_specs=specs if isinstance(out_shape, (list, tuple)) else specs[0],
         scratch_shapes=list(scratch),
         compiler_params=pltpu.CompilerParams(vmem_limit_bytes=mib * MIB),
         cost_estimate=pl.CostEstimate(flops=flops, bytes_accessed=size, transcendentals=0),
     )(*args)
+
+
+def shift(x, axis, by):
+    return lax.ppermute(x, axis, [(i, (i + by) % 4) for i in range(4)])
+
+
+def exchange(blocks, axis):
+    return [blocks[0]] + [shift(blocks[k], axis, k) for k in (1, 2, 3)]
+
+
+def collect(me, refs, held):
+    for k, ref in enumerate(refs):
+        held[(me - k) & 3] = ref[...]
 
 
 def low_half(shape):
@@ -79,7 +95,8 @@
     return jnp.transpose(jnp.broadcast_to(row, (128, 128)))
 
 
-def routing_kernel(ids_ref, place_ref, request_ref, slot_ref):
+def routing_kernel(me_ref, a_ref, b_ref, c_ref, d_ref, place_ref, request_ref, slot_ref, held):
+    collect(me_ref[0], (a_ref, b_ref, c_ref, d_ref), held)
     place = place_ref[...]
     lists = place.shape[1]
     lane = iota((128, 128), 1)
@@ -91,8 +108,8 @@
     before = (iota((128, 128), 1) < iota((128, 128), 0)).astype(F32).astype(BF)
     carry = jnp.zeros((1, 128), F32)
     request = jnp.zeros((128, 128), F32)
-    for q in range(ids_ref.shape[0]):
-        ids = as_column(ids_ref[q : q + 1, :])
+    for q in range(slot_ref.shape[0]):
+        ids = as_column(held[q // 2, q % 2 : q % 2 + 1, :])
         list_id = ids >> 8
         chosen = jnp.concatenate(
             [(list_id == lane + 128 * t).astype(F32).astype(BF) for t in range(lists // 128)], axis=1
@@ -140,20 +157,22 @@
                 out_ref[part * k + r + i] = pack(rows[at : at + CAP], CAP // 2)
 
 
-def pieces_kernel(slot_ref, fetched_ref, out_ref):
+def pieces_kernel(me_ref, slot_ref, fetched_ref, *out_refs):
     fetched = unpack(fetched_ref[...])
     slots = fetched.shape[0]
-    for m in range(out_ref.shape[0]):
-        column = jnp.concatenate([as_column(slot_ref[2 * m + i : 2 * m + i + 1, :]) for i in (0, 1)], axis=0)
+    for k, out_ref in enumerate(out_refs):
+        m = (me_ref[0] + k) & 3
+        column = jnp.concatenate([as_column(slot_ref[pl.ds(2 * m + i, 1), :]) for i in (0, 1)], axis=0)
         lane = iota((256, 128), 1)
         chosen = jnp.concatenate(
             [(column == lane + 128 * t).astype(F32).astype(BF) for t in range(slots // 128)], axis=1
         )
-        out_ref[m] = pack(dot(chosen, fetched), 128)
-
-
-def slots_kernel(slot_ref, grads_ref, out_ref):
-    grads = unpack(grads_ref[...])
+        out_ref[...] = pack(dot(chosen, fetched), 128)
+
+
+def slots_kernel(me_ref, slot_ref, a_ref, b_ref, c_ref, d_ref, out_ref, held):
+    collect(me_ref[0], (a_ref, b_ref, c_ref, d_ref), held)
+    grads = unpack(held[...])
     groups = out_ref.shape[0]
     step = 16 * CAP
     for r in range(0, groups * CAP, step):
@@ -191,8 +210,11 @@
 
 
 def step_kernel(
-    core_ref,
-    rows_ref,
+    me_ref,
+    a_ref,
+    b_ref,
+    c_ref,
+    d_ref,
     query_ref,
     labels_ref,
     wq_ref,
@@ -203,14 +225,24 @@
     gain_score_ref,
     w_score_ref,
     losses_ref,
-    base_ref,
     query_grad_ref,
-    keep_ref,
-    send_ref,
+    base_0_ref,
+    base_1_ref,
+    base_2_ref,
+    base_3_ref,
+    input_ref,
+    diff_q_ref,
+    diff_k_ref,
+    diff_v_ref,
+    context_ref,
+    diff_low_ref,
+    vectors_ref,
+    held,
     scores_t,
     attend_t,
-    grads,
 ):
+    me = me_ref[0]
+    collect(me, (a_ref, b_ref, c_ref, d_ref), held)
     queries, width = query_ref.shape
     size = 128
     head = width // HEADS
@@ -219,9 +251,9 @@
     low = low_half((size, 128))
 
     parts = []
-    for m in range(rows_ref.shape[0]):
-        main = rows_ref[m, :256, :].astype(F32)
-        tail = rows_ref[m, 256:, :].astype(F32)
+    for m in range(4):
+        main = held[m, :256, :].astype(F32)
+        tail = held[m, 256:, :].astype(F32)
         parts += [main, jnp.concatenate([tail[:, :64], tail[:, 64:]], axis=0)]
     rows_in = jnp.concatenate(parts, axis=1)
     vecs = query_ref[...].astype(F32)
@@ -314,26 +346,44 @@
     diff_base = diff_mixed + (diff_first - normed_one * lane_mean(diff_first * normed_one)) * inv_one
     for q in range(queries):
         query_grad_ref[q : q + 1, :] = jnp.sum(diff_base[size * q : size * (q + 1)], 0, keepdims=True)
-    for m in range(base_ref.shape[0]):
+    for m in range(4):
         slab = diff_base[:, SLAB * m : SLAB * (m + 1)]
-        base_ref[m, :256, :] = slab[:, :128].astype(BF)
-        base_ref[m, 256:, :] = jnp.concatenate([slab[:128, 128:], slab[128:, 128:]], axis=1).astype(BF)
-
-    grads[0] = dot(first_input, diff_q, 0, 0)
-    grads[1] = dot(first_input, diff_k, 0, 0)
-    grads[2] = dot(first_input, diff_v, 0, 0)
-    grads[3] = dot(context, diff_low, 0, 0)
+        held[m, :256, :] = slab[:, :128].astype(BF)
+        held[m, 256:, :] = jnp.concatenate([slab[:128, 128:], slab[128:, 128:]], axis=1).astype(BF)
+    for k, ref in enumerate((base_0_ref, base_1_ref, base_2_ref, base_3_ref)):
+        ref[...] = held[(me + k) & 3]
+    input_ref[...] = first_input
+    diff_q_ref[...] = diff_q
+    diff_k_ref[...] = diff_k
+    diff_v_ref[...] = diff_v
+    context_ref[...] = context
+    diff_low_ref[...] = diff_low
     vectors = [
         v[:, 128 * t : 128 * (t + 1)]
         for v in (grad_gain_attn, grad_gain_score, grad_w_score)
         for t in range(width // 128)
     ]
-    vectors = jnp.concatenate(vectors + [jnp.zeros((32 - len(vectors), 128), F32)], axis=0)
+    vectors_ref[...] = jnp.concatenate(vectors + [jnp.zeros((32 - len(vectors), 128), F32)], axis=0)
+
+
+FIRST = 48
+
+
+def gradients_kernel(
+    core_ref, input_ref, diff_q_ref, diff_k_ref, diff_v_ref, context_ref, diff_low_ref, vectors_ref,
+    keep_x_ref, send_x_ref, keep_y_ref, send_y_ref, grads,
+):
+    first_input = input_ref[...]
+    grads[0] = dot(first_input, diff_q_ref[...], 0, 0)
+    grads[1] = dot(first_input, diff_k_ref[...], 0, 0)
+    grads[2] = dot(first_input, diff_v_ref[...], 0, 0)
+    grads[3] = dot(context_ref[...], diff_low_ref[...], 0, 0)
     first_core = core_ref[0] == 0
 
     def assemble(at, carry):
         chunk = [grads[i, pl.ds(pl.multiple_of(24 * at, 8), 24), :] for i in range(4)]
         halves = [jnp.concatenate([g[12 * c : 12 * (c + 1)] for g in chunk], axis=0) for c in (0, 1)]
+        y, z = at >> 3, at & 7
         for m in range(4):
             blocks = []
             for rows48 in halves:
@@ -341,16 +391,79 @@
                 for h in range(9 * m, 9 * m + 9):
                     rb, t = h // 6, h % 6
                     tiles.append(rows48[8 * rb : 8 * rb + 8, 128 * t : 128 * (t + 1)])
-                blocks.append(jnp.concatenate(tiles + [vectors[8 * m : 8 * m + 8]], axis=0).astype(BF))
-            keep_ref[m, at] = jnp.where(first_core, blocks[0], blocks[1])
-            send_ref[m, at] = jnp.where(first_core, blocks[1], blocks[0])
+                tiles.append(vectors_ref[8 * m : 8 * m + 8, :])
+                blocks.append(jnp.concatenate(tiles, axis=0).astype(BF))
+            keep = jnp.where(first_core, blocks[0], blocks[1])
+            send = jnp.where(first_core, blocks[1], blocks[0])
+            keep_x_ref[m, at] = keep[:FIRST]
+            send_x_ref[m, at] = send[:FIRST]
+            keep_y_ref[y, 8 * m + z] = keep[FIRST:]
+            send_y_ref[y, 8 * m + z] = send[FIRST:]
         return carry
 
-    lax.fori_loop(0, keep_ref.shape[1], assemble, 0)
-
-
-def finish_kernel(blocks_ref, q_ref, k_ref, v_ref, o_ref, vec_ref):
-    blocks = blocks_ref[...].astype(F32)
+    lax.fori_loop(0, keep_x_ref.shape[1], assemble, 0)
+
+
+def plus(*refs):
+    total = refs[0].astype(F32)
+    for r in refs[1:]:
+        total = total + r.astype(F32)
+    return total.astype(BF)
+
+
+def cores_kernel(me_ref, keep_ref, other_ref, own_ref, right_ref, left_ref, far_a_ref, far_b_ref):
+    me = me_ref[0]
+    n = far_a_ref.shape[0]
+
+    def add(i, carry):
+        for k, ref in ((0, own_ref), (1, right_ref), (3, left_ref)):
+            at = (me + k) & 3
+            ref[i] = plus(keep_ref[at, i], other_ref[at, i])
+            ref[i + n] = plus(keep_ref[at, i + n], other_ref[at, i + n])
+        at = (me + 2) & 3
+        far_a_ref[i] = plus(keep_ref[at, i], other_ref[at, i])
+        far_b_ref[i] = plus(keep_ref[at, i + n], other_ref[at, i + n])
+        return carry
+
+    lax.fori_loop(0, n, add, 0)
+
+
+def passing_kernel(right_ref, left_ref, far_a_ref, far_b_ref, right_out, left_out):
+    n = far_a_ref.shape[0]
+    right_out[:n] = plus(right_ref[:n], far_a_ref[...])
+    right_out[n:] = right_ref[n:]
+    left_out[:n] = left_ref[:n]
+    left_out[n:] = plus(left_ref[n:], far_b_ref[...])
+
+
+def three_kernel(a_ref, b_ref, c_ref, out_ref):
+    out_ref[...] = plus(a_ref[...], b_ref[...], c_ref[...])
+
+
+def last_kernel(a_ref, b_ref, out_ref):
+    for ref, at in ((a_ref, 0), (b_ref, FIRST)):
+        total = ref[0].astype(F32)
+        for i in range(1, ref.shape[0]):
+            total = total + ref[i].astype(F32)
+        out_ref[at : at + ref.shape[1], :] = total.astype(BF)
+
+
+def ring_sum(me, keep, other, axis):
+    _, n, rows, _ = keep.shape
+    block, half = shape((n, rows, 128)), shape((n // 2, rows, 128))
+    size = n * rows * 128 * 2
+    own, right, left, far_a, far_b = call(
+        cores_kernel, [block, block, block, half, half], (me, keep, other), 24, size, 12 * size, scalar=True
+    )
+    far_a, far_b = shift(far_a, axis, 1), shift(far_b, axis, 3)
+    right, left = call(passing_kernel, [block, block], (right, left, far_a, far_b), 16, size, 5 * size)
+    right, left = shift(right, axis, 1), shift(left, axis, 3)
+    return call(three_kernel, block, (own, right, left), 16, size, 4 * size)
+
+
+def finish_kernel(me_ref, a_ref, b_ref, c_ref, d_ref, q_ref, k_ref, v_ref, o_ref, vec_ref, held):
+    collect(me_ref[0], (a_ref, b_ref, c_ref, d_ref), held)
+    blocks = held[...].astype(F32)
     tiles = [blocks[m, 8 * i : 8 * i + 8] for m in range(4) for i in range(9)]
     rows48 = jnp.concatenate([jnp.concatenate(tiles[6 * rb : 6 * rb + 6], axis=1) for rb in range(6)], axis=0)
     for i, ref in enumerate((q_ref, k_ref, v_ref, o_ref)):
@@ -388,50 +501,52 @@
     n_yz = lax.axis_size(("y", "z"))
     slots = n_dp * CAP
 
-    ids = lax.all_gather(cand_item, "x", axis=0, tiled=True)
+    along_x = lax.axis_index("x").astype(jnp.int32).reshape(1)
+    along_y = lax.axis_index("y").astype(jnp.int32).reshape(1)
+    core = lax.axis_index("c").astype(jnp.int32).reshape(1)
+
+    ids = exchange([cand_item] * 4, "x")
     request, slot = call(
         routing_kernel,
         [shape((n_dp, CAP), jnp.int32), shape((n_mp * queries, size), jnp.int32)],
-        (ids, list_place.reshape(1, -1)),
-        24, 3 * 10**8, 10**6,
+        (along_x, *ids, list_place.reshape(1, -1)),
+        24, 3 * 10**8, 10**6, [pltpu.VMEM((n_mp, queries, size), jnp.int32)], True,
     )
     asked = swap(request, ROWS)
     found = call(
         owner_kernel, shape((n_dp, 48, 128)), (asked, item_table), 40, 2 * 10**9, 2 * 10**6
     )
     fetched = swap(found, ROWS)
-    pieces = call(pieces_kernel, shape((n_mp, 384, 128)), (slot, fetched), 40, 10**9, 2 * 10**6)
-    rows_in = swap(pieces, "x")
-    core = lax.axis_index("c").astype(jnp.int32).reshape(1)
-    args = (
-        core, rows_in, query_vec, labels,
-        query_weight, key_weight, value_weight, output_weight,
-        gain_attn.reshape(1, -1), gain_score.reshape(1, -1), w_score.reshape(1, -1),
-    )
-    outs = [
-        shape((queries, 128), F32),
-        shape((n_mp, 384, 128)),
-        shape((queries, width), F32),
-        shape((n_mp, n_yz, 80, 128)),
-        shape((n_mp, n_yz, 80, 128)),
-    ]
-    losses, diff_base, query_grad, keep, send = pl.pallas_call(
+    pieces = call(
+        pieces_kernel, [shape((384, 128))] * n_mp, (along_x, slot, fetched), 40, 10**9, 2 * 10**6, (), True
+    )
+    rows_in = exchange(pieces, "x")
+    acts = shape((queries * size, width))
+    outs = call(
         step_kernel,
-        out_shape=outs,
-        in_specs=[pl.BlockSpec(memory_space=pltpu.SMEM)] + whole(len(args) - 1),
-        out_specs=whole(len(outs)),
-        scratch_shapes=[
+        [shape((queries, 128), F32), shape((queries, width), F32)]
+        + [shape((384, 128))] * n_mp
+        + [acts] * 6
+        + [shape((32, 128), F32)],
+        (
+            along_x, *rows_in, query_vec, labels,
+            query_weight, key_weight, value_weight, output_weight,
+            gain_attn.reshape(1, -1), gain_score.reshape(1, -1), w_score.reshape(1, -1),
+        ),
+        48, 4 * 10**9, 10**7,
+        [
+            pltpu.VMEM((n_mp, 384, 128), BF),
             pltpu.VMEM((HEADS * queries // 2, 128, 256), F32),
             pltpu.VMEM((HEADS * queries // 2, 128, 256), F32),
-            pltpu.VMEM((4, width, width), F32),
         ],
-        compiler_params=pltpu.CompilerParams(vmem_limit_bytes=56 * MIB),
-        cost_estimate=pl.CostEstimate(flops=5 * 10**9, bytes_accessed=12 * 10**6, transcendentals=0),
-    )(*args)
-
-    column_grads = swap(diff_base, "x")
+        True,
+    )
+    losses, query_grad, diff_base, kept = outs[0], outs[1], outs[2:6], outs[6:]
+
+    column_grads = exchange(diff_base, "x")
     outgoing = call(
-        slots_kernel, shape((n_dp, 48, 128)), (slot, column_grads), 40, 10**9, 2 * 10**6
+        slots_kernel, shape((n_dp, 48, 128)), (along_x, slot, *column_grads), 40, 10**9, 2 * 10**6,
+        [pltpu.VMEM((n_mp, 384, 128), BF)], True,
     )
     arrived = swap(outgoing, ROWS)
     table_grad = call(
@@ -441,20 +556,24 @@
         40, 2 * 10**9, 4 * 10**6,
     )
 
-    other = lax.ppermute(send, "c", [(0, 1), (1, 0)])
-    both = (keep.astype(F32) + other.astype(F32)).astype(BF)
-
-    def summed(x):
-        return jnp.sum(x.astype(F32), 0).astype(BF)
-
-    over_x = summed(swap(both, "x"))
-    over_all = summed(swap(over_x, ("y", "z")))
-    blocks = lax.all_gather(over_all, "x", axis=0, tiled=False)
+    first, second = shape((4, n_yz, FIRST, 128)), shape((4, n_yz, 80 - FIRST, 128))
+    keep_x, send_x, keep_y, send_y = call(
+        gradients_kernel, [first, first, second, second], (core, *kept), 48, 2 * 10**9, 10**7,
+        [pltpu.VMEM((4, width, width), F32)], True,
+    )
+    other_x = lax.ppermute(send_x, "c", [(0, 1), (1, 0)])
+    other_y = lax.ppermute(send_y, "c", [(0, 1), (1, 0)])
+    over_x = ring_sum(along_x, keep_x, other_x, "x")
+    over_y = ring_sum(along_y, keep_y, other_y, "y")
+    parts_x = swap(over_x, ("y", "z"))
+    parts_y = swap(over_y, ("x", "z"))
+    over_all = call(last_kernel, shape((80, 128)), (parts_x, parts_y), 8, 10**6, 10**6)
+    blocks = exchange([over_all] * 4, "x")
     rows = width // n_dp
     finished = call(
         finish_kernel,
         [shape((rows, width), F32)] * 4 + [shape((32, 128), F32)],
-        (blocks,), 8, 10**6, 10**6,
+        (along_x, *blocks), 8, 10**6, 10**6, [pltpu.VMEM((n_mp, 80, 128), BF)], True,
     )
     vectors = finished[4].reshape(-1)
     return (

time: 215 us -> 213 us (level)
  the two profiles are of different devices: /device:TPU:32 before, /device:TPU:1 now
where the time goes in v2:
time: 213 us; the launch traced here: 210 us
  starting transfers between devices  80 us (38%)
  waiting for transfers between devices  55.2 us (26%)
  Pallas kernels  32.8 us (15%)
  blocking collectives  27 us (13%)
  local copies, waits for them, and re-layouts  12.6 us (6%)
    all_to_all x4, starting transfers between devices, swap(): return lax.all_to_all(x, axes, split_axis=0, concat_axis=0, tiled=True)  41.4 us
    ppermute x20, starting transfers between devices, shift(): return lax.ppermute(x, axis, [(i, (i + by) % 4) for i in range(4)])  37.4 us
    pallas_call x15, Pallas kernels, call(): pl.pallas_call(kernel, out_shape=out_shape, in_specs=in_specs, out_specs=...  32.8 us
    all_to_all x4, waiting for transfers between devices, swap(): return lax.all_to_all(x, axes, split_axis=0, concat_axis=0, tiled=True)  27.4 us
    all_to_all x1, blocking collectives, swap(): return lax.all_to_all(x, axes, split_axis=0, concat_axis=0, tiled=True)  27 us
    ppermute x20, waiting for transfers between devices, shift(): return lax.ppermute(x, axis, [(i, (i + by) % 4) for i in range(4)])  23.1 us
    unnamed x58, local copies, waits for them, and re-layouts  10.8 us
    ppermute x1, waiting for transfers between devices, body(): other_y = lax.ppermute(send_y, 'c', [(0, 1), (1, 0)])  4.74 us
  transfers between devices with their start and end apart: 26, of which 13 were waited for; matrix products, arithmetic and copies ran while one was open for 2% of the time, Pallas kernels for 4%

profile of v2, /device:TPU:1, one launch (start us, length us, event | category | flops | bytes accessed | tf_op | source)
XLA Modules:
  0.0 209.6 jit_solution(3234475878171462363)
XLA Ops:
  0.6 2.1 %collective-permute-start = (s32[2,128]{1,0:T(2,128)}, s32[2,128]{1,0:T(2,128)S(1)}, u32[]{:S(2)}, u32[]{:S(2)}) collective-permute-start(s32[2,128]{1,0:T(2,128)} %a_ref.1), channel_id=1, source_target_pairs={{0,1},{1,2},{2,3},{3,0},{4,5},{5,6},{6,7},{7,4},{8,9},{9,10},{10,1... | collective-permute-start | bytes 3080 | tf_op jit(solution)/shard_map/ppermute | solution.py:53
  2.8 2.5 %collective-permute-start.1 = (s32[2,128]{1,0:T(2,128)}, s32[2,128]{1,0:T(2,128)S(1)}, u32[]{:S(2)}, u32[]{:S(2)}) collective-permute-start(s32[2,128]{1,0:T(2,128)} %a_ref.1), channel_id=1, source_target_pairs={{0,2},{1,3},{2,0},{3,1},{4,6},{5,7},{6,4},{7,5},{8,10},{9,11},{10,... | collective-permute-start | bytes 3080 | tf_op jit(solution)/shard_map/ppermute | solution.py:53
  5.2 1.2 collective-permute-start.2
  6.4 0.5 collective-permute-done.1.c_ref
  6.9 1.2 collective-permute-done.2.d_ref
  8.1 0.7 copy-done.17
  8.8 0.7 copy-done.18
  9.5 3.4 %shard_map.195 = (s32[64,32]{1,0:T(8,128)}, s32[8,128]{1,0:T(8,128)S(1)}) custom-call(s32[1]{0:T(128)} %bitcast.me_ref, s32[2,128]{1,0:T(2,128)S(1)} %copy-done.18, s32[2,128]{1,0:T(2,128)S(1)} %collective-permute-done.b_ref, s32[2,128]{1,0:T(2,128)S(1)} %collective-permute-done.1.c_ref, s32[2,128]{1,0:T(2,128)S(1)} %collective-permute-done.2.d_ref, ...), custom_call_target="tpu_custom_call" | custom-call | flops 300000000 | bytes 1000000 | tf_op jit(solution)/shard_map/pallas_call | solution.py:41
  12.9 13.7 %all-to-all-start = ((s32[64,1,32]{2,1,0:T(1,128)}), s32[64,1,32]{2,1,0:T(1,128)S(1)}, u32[]{:S(2)}, u32[]{:S(2)}) async-start(s32[64,1,32]{2,1,0:T(1,128)} %bitcast.3), calls=%async_computation | async-start | bytes 65536 | tf_op jit(solution)/shard_map/all_to_all | solution.py:479
  26.7 0.5 copy.27.table_ref
  27.2 8.7 %all-to-all-done = s32[64,1,32]{2,1,0:T(1,128)S(1)} async-done(((s32[64,1,32]{2,1,0:T(1,128)}), s32[64,1,32]{2,1,0:T(1,128)S(1)}, u32[]{:S(2)}, u32[]{:S(2)}) %all-to-all-start) | async-done | bytes 8224 | tf_op jit(solution)/shard_map/all_to_all | solution.py:479
  35.9 2.5 %shard_map.196 = bf16[64,48,128]{2,1,0:T(8,128)(2,1)S(1)} custom-call(s32[64,32]{1,0:T(8,128)S(1)} %bitcast.14, bf16[2048,192]{1,0:T(8,128)(2,1)S(1)} %copy.27.table_ref), custom_call_target="tpu_custom_call" | custom-call | flops 2000000000 | bytes 2000000 | tf_op jit(solution)/shard_map/pallas_call | solution.py:41
  38.4 27.0 %all_to_all.31.fetched_ref = bf16[64,48,128]{2,1,0:T(8,128)(2,1)S(1)} all-to-all(bf16[64,48,128]{2,1,0:T(8,128)(2,1)S(1)} %shard_map.196), channel_id=1, replica_groups=mesh['y'=4,'z'=8,'c'=2,'x'=4] {'y','z','c'}, dimensions={0} | all-to-all | bytes 1572864 | tf_op jit(solution)/shard_map/all_to_all | solution.py:479
  65.5 1.4 shard_map.197
  66.9 0.6 copy-done.22
  67.5 3.5 %collective-permute-start.4 = (bf16[384,128]{1,0:T(8,128)(2,1)S(1)}, bf16[384,128]{1,0:T(8,128)(2,1)S(1)}, u32[]{:S(2)}, u32[]{:S(2)}) collective-permute-start(bf16[384,128]{1,0:T(8,128)(2,1)S(1)} %get-tuple-element.56), channel_id=1, source_target_pairs={{0,2},{1,3},{2,0},{3,1},{4,6},{5,7},{6,4},{7,5},{8,10},{9,11},{10,... | collective-permute-start | bytes 294920 | tf_op jit(solution)/shard_map/ppermute | solution.py:53
  71.4 1.3 collective-permute-done.3.b_ref
  72.7 3.0 %collective-permute-done.4.c_ref = bf16[384,128]{1,0:T(8,128)(2,1)S(1)} collective-permute-done((bf16[384,128]{1,0:T(8,128)(2,1)S(1)}, bf16[384,128]{1,0:T(8,128)(2,1)S(1)}, u32[]{:S(2)}, u32[]{:S(2)}) %collective-permute-start.4) | collective-permute-done | bytes 98336 | tf_op jit(solution)/shard_map/ppermute | solution.py:53
  75.7 0.9 copy-done.23
  76.6 11.1 %shard_map.198 = (f32[2,128]{1,0:T(2,128)S(1)}, f32[2,768]{1,0:T(2,128)}, bf16[384,128]{1,0:T(8,128)(2,1)S(1)}, bf16[384,128]{1,0:T(8,128)(2,1)S(1)}, bf16[384,1...) custom-call(s32[1]{0:T(128)} %bitcast.me_ref, ...), custom_call_target="tpu_custom_call" | custom-call | flops 4000000000 | bytes 10000000 | tf_op jit(solution)/shard_map/pallas_call | solution.py:41
  87.7 0.6 copy-done.10
  88.4 0.6 copy-done.12
  89.0 0.6 copy-done.14
  89.7 4.3 %shard_map.201 = (bf16[4,32,48,128]{3,2,1,0:T(8,128)(2,1)S(1)}, bf16[4,32,48,128]{3,2,1,0:T(8,128)(2,1)}, bf16[4,32,32,128]{3,2,1,0:T(8,128)(2,1)S(1)}, bf16[4,32,32,128]{3,2,1,0:T(8,128)(2,1)}) custom-call(s32[1]{0:T(128)} %bitcast.5.core_ref, bf16[256,768]{1,0:T(8,128)(2,1)S(1)} %get-tuple-element.64.input_ref, ...), custom_call_target="tpu_custom_call" | custom-call | flops 2000000000 | bytes 10000000 | tf_op jit(solution)/shard_map/pallas_call | solution.py:41
  93.9 1.0 copy-done
  94.9 1.2 collective-permute-start.9
  96.2 4.7 %collective-permute-done.14.other_ref = bf16[4,32,32,128]{3,2,1,0:T(8,128)(2,1)} collective-permute-done((bf16[4,32,32,128]{3,2,1,0:T(8,128)(2,1)}, bf16[4,32,32,128]{3,2,1,0:T(8,128)(2,1)}, u32[]{:S(2)}, u32[]{:S(2)}) %collective-permute-start.14) | collective-permute-done | bytes 1048608 | tf_op jit(solution)/shard_map/ppermute | solution.py:565
  100.9 1.2 copy-done.1
  102.1 1.5 shard_map.205
  103.7 1.3 collective-permute-start.15
  105.0 1.5 collective-permute-start.16
  106.5 3.4 %collective-permute-done.15.far_a_ref = bf16[16,32,128]{2,1,0:T(8,128)(2,1)S(1)} collective-permute-done((bf16[16,32,128]{2,1,0:T(8,128)(2,1)S(1)}, bf16[16,32,128]{2,1,0:T(8,128)(2,1)S(1)}, u32[]{:S(2)}, u32[]{:S(2)}) %collective-permute-start.15) | collective-permute-done | bytes 131104 | tf_op jit(solution)/shard_map/ppermute | solution.py:53
  110.0 10.5 %collective-permute-start.17 = (bf16[32,32,128]{2,1,0:T(8,128)(2,1)S(1)}, bf16[32,32,128]{2,1,0:T(8,128)(2,1)S(1)}, u32[]{:S(2)}, u32[]{:S(2)}) collective-permute-start(bf16[32,32,128]{2,1,0:T(8,128)(2,1)S(1)} %get-tuple-element.87), channel_id=1, source_target_pairs={{0,64},{64,128},{128,192},{192,0},{1,65},{65,129},{129,193},{193,1... | collective-permute-start | bytes 786440 | tf_op jit(solution)/shard_map/ppermute | solution.py:53
  120.5 2.0 collective-permute-start.18
  122.5 1.2 shard_map.202
  123.7 0.7 copy-done.2
  124.4 0.7 copy-done.4
  125.2 0.3 collective-permute-start.10
  125.5 2.3 %collective-permute-start.11 = (bf16[16,48,128]{2,1,0:T(8,128)(2,1)}, bf16[16,48,128]{2,1,0:T(8,128)(2,1)S(1)}, u32[]{:S(2)}, u32[]{:S(2)}) collective-permute-start(bf16[16,48,128]{2,1,0:T(8,128)(2,1)} %get-tuple-element.77), channel_id=1, source_target_pairs={{0,3},{1,0},{2,1},{3,2},{4,7},{5,4},{6,5},{7,6},{8,11},{9,8},{10,9... | collective-permute-start | bytes 589832 | tf_op jit(solution)/shard_map/ppermute | solution.py:53
  127.9 0.8 shard_map.207
  128.7 6.2 %all-to-all-start.4 = ((bf16[32,32,128]{2,1,0:T(8,128)(2,1)}), bf16[32,32,128]{2,1,0:T(8,128)(2,1)S(1)}, u32[]{:S(2)}, u32[]{:S(2)}) async-start(bf16[32,32,128]{2,1,0:T(8,128)(2,1)} %shard_map.207), calls=%async_computation.4 | async-start | bytes 524288 | tf_op jit(solution)/shard_map/all_to_all | solution.py:479
  135.0 1.3 collective-permute-start.12
  136.3 1.4 collective-permute-start.13
  137.8 10.4 %collective-permute-done.12.b_ref = bf16[32,48,128]{2,1,0:T(8,128)(2,1)S(1)} collective-permute-done((bf16[32,48,128]{2,1,0:T(8,128)(2,1)S(1)}, bf16[32,48,128]{2,1,0:T(8,128)(2,1)S(1)}, u32[]{:S(2)}, u32[]{:S(2)}) %collective-permute-start.12) | collective-permute-done | bytes 393248 | tf_op jit(solution)/shard_map/ppermute | solution.py:53
  148.3 0.9 shard_map.204
  149.2 8.9 %all-to-all-start.3 = ((bf16[32,48,128]{2,1,0:T(8,128)(2,1)}), bf16[32,48,128]{2,1,0:T(8,128)(2,1)S(1)}, u32[]{:S(2)}, u32[]{:S(2)}) async-start(bf16[32,48,128]{2,1,0:T(8,128)(2,1)} %shard_map.204), calls=%async_computation.3 | async-start | bytes 786432 | tf_op jit(solution)/shard_map/all_to_all | solution.py:479
  158.1 0.4 collective-permute-start.6
  158.5 2.3 %collective-permute-start.7 = (bf16[384,128]{1,0:T(8,128)(2,1)S(1)}, bf16[384,128]{1,0:T(8,128)(2,1)S(1)}, u32[]{:S(2)}, u32[]{:S(2)}) collective-permute-start(bf16[384,128]{1,0:T(8,128)(2,1)S(1)} %copy-done.13), channel_id=1, source_target_pairs={{0,2},{1,3},{2,0},{3,1},{4,6},{5,7},{6,4},{7,5},{8,10},{9,11},{10,... | collective-permute-start | bytes 294920 | tf_op jit(solution)/shard_map/ppermute | solution.py:53
  160.8 0.9 collective-permute-start.8
  161.7 2.2 %collective-permute-done.6.b_ref = bf16[384,128]{1,0:T(8,128)(2,1)S(1)} collective-permute-done((bf16[384,128]{1,0:T(8,128)(2,1)S(1)}, bf16[384,128]{1,0:T(8,128)(2,1)S(1)}, u32[]{:S(2)}, u32[]{:S(2)}) %collective-permute-start.6) | collective-permute-done | bytes 98336 | tf_op jit(solution)/shard_map/ppermute | solution.py:53
  163.9 0.9 collective-permute-done.8.d_ref
  164.8 2.2 %shard_map.199 = bf16[64,48,128]{2,1,0:T(8,128)(2,1)} custom-call(s32[1]{0:T(128)} %bitcast.me_ref, s32[8,128]{1,0:T(8,128)S(1)} %get-tuple-element.52.slot_ref, bf16[384,128]{1,0:T(8,128)(2,1)S(1)} %copy-done.21, bf16[384,128]{1,0:T(8,128)(2,1)S(1)} %collective-permute-done.6.b_ref, bf16[384,128]{1,0:T(8,128)(2,1)S(1)} %collective-permute-done.7.c_ref, ...), custom_call_target="tpu_custom_call" | custom-call | flops 1000000000 | bytes 2000000 | tf_op jit(solution)/shard_map/pallas_call | solution.py:41
  167.1 1.3 all-to-all-done.3.a_ref
  168.4 12.6 %all-to-all-start.2 = ((bf16[64,48,128]{2,1,0:T(8,128)(2,1)}), bf16[64,48,128]{2,1,0:T(8,128)(2,1)S(1)}, u32[]{:S(2)}, u32[]{:S(2)}) async-start(bf16[64,48,128]{2,1,0:T(8,128)(2,1)} %shard_map.199), calls=%async_computation.2 | async-start | bytes 1572864 | tf_op jit(solution)/shard_map/all_to_all | solution.py:479
  181.0 0.5 broadcast.4
  181.5 0.7 reduce.5
  182.3 0.6 slice_reduce_fusion
  183.0 0.9 collective-permute-start.19
  183.9 2.5 %collective-permute-start.20 = (bf16[80,128]{1,0:T(8,128)(2,1)S(1)}, bf16[80,128]{1,0:T(8,128)(2,1)S(1)}, u32[]{:S(2)}, u32[]{:S(2)}) collective-permute-start(bf16[80,128]{1,0:T(8,128)(2,1)S(1)} %shard_map.208.a_ref), channel_id=1, source_target_pairs={{0,2},{1,3},{2,0},{3,1},{4,6},{5,7},{6,4},{7,5},{8,10},{9,11},{10,... | collective-permute-start | bytes 61448 | tf_op jit(solution)/shard_map/ppermute | solution.py:53
  186.6 17.4 %all-to-all-done.2.arrived_ref = bf16[64,48,128]{2,1,0:T(8,128)(2,1)S(1)} async-done(((bf16[64,48,128]{2,1,0:T(8,128)(2,1)}), bf16[64,48,128]{2,1,0:T(8,128)(2,1)S(1)}, u32[]{:S(2)}, u32[]{:S(2)}) %all-to-all-start.2) | async-done | bytes 786464 | tf_op jit(solution)/shard_map/all_to_all | solution.py:479
  204.0 2.4 %shard_map.200 = f32[2048,192]{1,0:T(8,128)S(1)} custom-call(s32[16,128]{1,0:T(8,128)S(1)} %reshape.56.asked_ref, bf16[64,48,128]{2,1,0:T(8,128)(2,1)S(1)} %all-to-all-done.2.arrived_ref), custom_call_target="tpu_custom_call" | custom-call | flops 2000000000 | bytes 4000000 | tf_op jit(solution)/shard_map/pallas_call | solution.py:41
  206.4 1.7 copy.28
  208.1 0.7 shard_map.209
  208.8 0.6 slice_bitcast_fusion
  (70 shorter events, 1.0 us)
Async XLA Ops:
  0.6 5.7 %collective-permute-start = (s32[2,128]{1,0:T(2,128)}, s32[2,128]{1,0:T(2,128)S(1)}, u32[]{:S(2)}, u32[]{:S(2)}) collective-permute-start(s32[2,128]{1,0:T(2,128)} %a_ref.1), channel_id=1, source_target_pairs={{0,1},{1,2},{2,3},{3,0},{4,5},{5,6},{6,7},{7,4},{8,9},{9,10},{10,1... | collective-permute-start | bytes 3080 | tf_op jit(solution)/shard_map/ppermute | solution.py:53
  2.8 4.1 %collective-permute-start.1 = (s32[2,128]{1,0:T(2,128)}, s32[2,128]{1,0:T(2,128)S(1)}, u32[]{:S(2)}, u32[]{:S(2)}) collective-permute-start(s32[2,128]{1,0:T(2,128)} %a_ref.1), channel_id=1, source_target_pairs={{0,2},{1,3},{2,0},{3,1},{4,6},{5,7},{6,4},{7,5},{8,10},{9,11},{10,... | collective-permute-start | bytes 3080 | tf_op jit(solution)/shard_map/ppermute | solution.py:53
  5.2 2.9 %collective-permute-start.2 = (s32[2,128]{1,0:T(2,128)}, s32[2,128]{1,0:T(2,128)S(1)}, u32[]{:S(2)}, u32[]{:S(2)}) collective-permute-start(s32[2,128]{1,0:T(2,128)} %a_ref.1), channel_id=1, source_target_pairs={{0,3},{1,0},{2,1},{3,2},{4,7},{5,4},{6,5},{7,6},{8,11},{9,8},{10,9... | collective-permute-start | bytes 3080 | tf_op jit(solution)/shard_map/ppermute | solution.py:53
  8.1 0.7 copy-start.17
  8.8 0.7 copy-start.18
  9.5 17.2 %copy-start.24 = (bf16[2048,192]{0,1:T(8,128)(2,1)S(1)}, bf16[2048,192]{0,1:T(8,128)(2,1)}, u32[]{:S(2)}) copy-start(bf16[2048,192]{0,1:T(8,128)(2,1)} %param.14) | copy-start | bytes 2359300
  12.9 23.0 %all-to-all-start = ((s32[64,1,32]{2,1,0:T(1,128)}), s32[64,1,32]{2,1,0:T(1,128)S(1)}, u32[]{:S(2)}, u32[]{:S(2)}) async-start(s32[64,1,32]{2,1,0:T(1,128)} %bitcast.3), calls=%async_computation | async-start | bytes 65536 | tf_op jit(solution)/shard_map/all_to_all | solution.py:479
  35.9 2.5 %copy-start.6 = (s32[64,1,32]{2,1,0:T(1,128)}, s32[64,1,32]{2,1,0:T(1,128)S(1)}, u32[]{:S(2)}) copy-start(s32[64,1,32]{2,1,0:T(1,128)S(1)} %all-to-all-done) | copy-start | bytes 24580
  65.4 5.9 %copy-start.25 = (f32[768]{0:T(1024)S(1)}, f32[768]{0:T(1024)}, u32[]{:S(2)}) copy-start(f32[768]{0:T(1024)} %param.21) | copy-start | bytes 9220
  65.4 5.9 %copy-start.26 = (f32[768]{0:T(1024)S(1)}, f32[768]{0:T(1024)}, u32[]{:S(2)}) copy-start(f32[768]{0:T(1024)} %param.22) | copy-start | bytes 9220
  65.4 5.9 %copy-start.27 = (f32[768]{0:T(1024)S(1)}, f32[768]{0:T(1024)}, u32[]{:S(2)}) copy-start(f32[768]{0:T(1024)} %param.23) | copy-start | bytes 9220
  65.4 10.3 %copy-start.8 = (bf16[768,768]{1,0:T(8,128)(2,1)S(1)}, bf16[768,768]{1,0:T(8,128)(2,1)}, u32[]{:S(2)}) copy-start(bf16[768,768]{1,0:T(8,128)(2,1)} %wq_ref.1) | copy-start | bytes 3538948
  65.4 10.3 %copy-start.9 = (bf16[768,768]{1,0:T(8,128)(2,1)S(1)}, bf16[768,768]{1,0:T(8,128)(2,1)}, u32[]{:S(2)}) copy-start(bf16[768,768]{1,0:T(8,128)(2,1)} %wk_ref.1) | copy-start | bytes 3538948
  65.5 10.3 %copy-start.16 = (bf16[2,768]{1,0:T(2,128)(2,1)S(1)}, bf16[2,768]{1,0:T(2,128)(2,1)}, u32[]{:S(2)}) copy-start(bf16[2,768]{1,0:T(2,128)(2,1)} %query_ref.1) | copy-start | bytes 9220
  65.5 10.2 %copy-start.19 = (s32[2,128]{1,0:T(2,128)S(1)}, s32[2,128]{1,0:T(2,128)}, u32[]{:S(2)}) copy-start(s32[2,128]{1,0:T(2,128)} %labels_ref.1) | copy-start | bytes 3076
  66.9 0.6 copy-start.22
  67.5 5.2 %collective-permute-start.3 = (bf16[384,128]{1,0:T(8,128)(2,1)S(1)}, bf16[384,128]{1,0:T(8,128)(2,1)S(1)}, u32[]{:S(2)}, u32[]{:S(2)}) collective-permute-start(bf16[384,128]{1,0:T(8,128)(2,1)S(1)} %get-tuple-element.55), channel_id=1, source_target_pairs={{0,1},{1,2},{2,3},{3,0},{4,5},{5,6},{6,7},{7,4},{8,9},{9,10},{10,1... | collective-permute-start | bytes 294920 | tf_op jit(solution)/shard_map/ppermute | solution.py:53
  67.5 8.2 %collective-permute-start.4 = (bf16[384,128]{1,0:T(8,128)(2,1)S(1)}, bf16[384,128]{1,0:T(8,128)(2,1)S(1)}, u32[]{:S(2)}, u32[]{:S(2)}) collective-permute-start(bf16[384,128]{1,0:T(8,128)(2,1)S(1)} %get-tuple-element.56), channel_id=1, source_target_pairs={{0,2},{1,3},{2,0},{3,1},{4,6},{5,7},{6,4},{7,5},{8,10},{9,11},{10,... | collective-permute-start | bytes 294920 | tf_op jit(solution)/shard_map/ppermute | solution.py:53
  71.1 4.6 %collective-permute-start.5 = (bf16[384,128]{1,0:T(8,128)(2,1)S(1)}, bf16[384,128]{1,0:T(8,128)(2,1)S(1)}, u32[]{:S(2)}, u32[]{:S(2)}) collective-permute-start(bf16[384,128]{1,0:T(8,128)(2,1)S(1)} %get-tuple-element.57), channel_id=1, source_target_pairs={{0,3},{1,0},{2,1},{3,2},{4,7},{5,4},{6,5},{7,6},{8,11},{9,8},{10,9... | collective-permute-start | bytes 294920 | tf_op jit(solution)/shard_map/ppermute | solution.py:53
  75.7 0.9 copy-start.23
  87.7 0.6 copy-start.10
  88.4 0.6 copy-start.12
  89.0 0.6 copy-start.14
  89.6 4.3 %copy-start.20 = (bf16[384,128]{1,0:T(8,128)(2,1)}, bf16[384,128]{1,0:T(8,128)(2,1)S(1)}, u32[]{:S(2)}) copy-start(bf16[384,128]{1,0:T(8,128)(2,1)S(1)} %get-tuple-element.59.a_ref) | copy-start | bytes 294916
  93.9 1.0 copy-start
  94.9 27.5 %collective-permute-start.9 = (bf16[4,32,48,128]{3,2,1,0:T(8,128)(2,1)}, bf16[4,32,48,128]{3,2,1,0:T(8,128)(2,1)S(1)}, u32[]{:S(2)}, u32[]{:S(2)}) collective-permute-start(bf16[4,32,48,128]{3,2,1,0:T(8,128)(2,1)} %get-tuple-element.72), channel_id=1, source_target_pairs={{0,4},{4,0},{1,5},{5,1},{2,6},{6,2},{3,7},{7,3},{8,12},{12,8},{9,1... | collective-permute-start | bytes 4718600 | tf_op jit(solution)/shard_map/ppermute | solution.py:564
  96.2 4.7 %collective-permute-start.14 = (bf16[4,32,32,128]{3,2,1,0:T(8,128)(2,1)}, bf16[4,32,32,128]{3,2,1,0:T(8,128)(2,1)}, u32[]{:S(2)}, u32[]{:S(2)}) collective-permute-start(bf16[4,32,32,128]{3,2,1,0:T(8,128)(2,1)} %get-tuple-element.81), channel_id=1, source_target_pairs={{0,4},{4,0},{1,5},{5,1},{2,6},{6,2},{3,7},{7,3},{8,12},{12,8},{9,1... | collective-permute-start | bytes 3145736 | tf_op jit(solution)/shard_map/ppermute | solution.py:565
  100.9 1.2 copy-start.1
  103.7 6.2 %collective-permute-start.15 = (bf16[16,32,128]{2,1,0:T(8,128)(2,1)S(1)}, bf16[16,32,128]{2,1,0:T(8,128)(2,1)S(1)}, u32[]{:S(2)}, u32[]{:S(2)}) collective-permute-start(bf16[16,32,128]{2,1,0:T(8,128)(2,1)S(1)} %get-tuple-element.85), channel_id=1, source_target_pairs={{0,64},{64,128},{128,192},{192,0},{1,65},{65,129},{129,193},{193,1... | collective-permute-start | bytes 393224 | tf_op jit(solution)/shard_map/ppermute | solution.py:53
  105.0 5.0 %collective-permute-start.16 = (bf16[16,32,128]{2,1,0:T(8,128)(2,1)S(1)}, bf16[16,32,128]{2,1,0:T(8,128)(2,1)S(1)}, u32[]{:S(2)}, u32[]{:S(2)}) collective-permute-start(bf16[16,32,128]{2,1,0:T(8,128)(2,1)S(1)} %get-tuple-element.86), channel_id=1, source_target_pairs={{0,192},{64,0},{128,64},{192,128},{1,193},{65,1},{129,65},{193,129... | collective-permute-start | bytes 393224 | tf_op jit(solution)/shard_map/ppermute | solution.py:53
  110.0 17.9 %collective-permute-start.17 = (bf16[32,32,128]{2,1,0:T(8,128)(2,1)S(1)}, bf16[32,32,128]{2,1,0:T(8,128)(2,1)S(1)}, u32[]{:S(2)}, u32[]{:S(2)}) collective-permute-start(bf16[32,32,128]{2,1,0:T(8,128)(2,1)S(1)} %get-tuple-element.87), channel_id=1, source_target_pairs={{0,64},{64,128},{128,192},{192,0},{1,65},{65,129},{129,193},{193,1... | collective-permute-start | bytes 786440 | tf_op jit(solution)/shard_map/ppermute | solution.py:53
  120.5 7.4 %collective-permute-start.18 = (bf16[32,32,128]{2,1,0:T(8,128)(2,1)S(1)}, bf16[32,32,128]{2,1,0:T(8,128)(2,1)S(1)}, u32[]{:S(2)}, u32[]{:S(2)}) collective-permute-start(bf16[32,32,128]{2,1,0:T(8,128)(2,1)S(1)} %get-tuple-element.88), channel_id=1, source_target_pairs={{0,192},{64,0},{128,64},{192,128},{1,193},{65,1},{129,65},{193,129... | collective-permute-start | bytes 786440 | tf_op jit(solution)/shard_map/ppermute | solution.py:53
  123.7 0.7 copy-start.2
  124.4 0.8 copy-start.4
  125.2 9.7 %copy-start.3 = (bf16[32,48,128]{2,1,0:T(8,128)(2,1)S(1)}, bf16[32,48,128]{2,1,0:T(8,128)(2,1)}, u32[]{:S(2)}) copy-start(bf16[32,48,128]{2,1,0:T(8,128)(2,1)} %copy-done.2) | copy-start | bytes 1179652
  125.2 9.7 %copy-start.5 = (bf16[32,48,128]{2,1,0:T(8,128)(2,1)S(1)}, bf16[32,48,128]{2,1,0:T(8,128)(2,1)}, u32[]{:S(2)}) copy-start(bf16[32,48,128]{2,1,0:T(8,128)(2,1)} %copy-done.4) | copy-start | bytes 1179652
  125.2 9.7 %collective-permute-start.10 = (bf16[16,48,128]{2,1,0:T(8,128)(2,1)}, bf16[16,48,128]{2,1,0:T(8,128)(2,1)S(1)}, u32[]{:S(2)}, u32[]{:S(2)}) collective-permute-start(bf16[16,48,128]{2,1,0:T(8,128)(2,1)} %get-tuple-element.76), channel_id=1, source_target_pairs={{0,1},{1,2},{2,3},{3,0},{4,5},{5,6},{6,7},{7,4},{8,9},{9,10},{10,1... | collective-permute-start | bytes 589832 | tf_op jit(solution)/shard_map/ppermute | solution.py:53
  125.5 9.3 %collective-permute-start.11 = (bf16[16,48,128]{2,1,0:T(8,128)(2,1)}, bf16[16,48,128]{2,1,0:T(8,128)(2,1)S(1)}, u32[]{:S(2)}, u32[]{:S(2)}) collective-permute-start(bf16[16,48,128]{2,1,0:T(8,128)(2,1)} %get-tuple-element.77), channel_id=1, source_target_pairs={{0,3},{1,0},{2,1},{3,2},{4,7},{5,4},{6,5},{7,6},{8,11},{9,8},{10,9... | collective-permute-start | bytes 589832 | tf_op jit(solution)/shard_map/ppermute | solution.py:53
  128.7 20.5 %all-to-all-start.4 = ((bf16[32,32,128]{2,1,0:T(8,128)(2,1)}), bf16[32,32,128]{2,1,0:T(8,128)(2,1)S(1)}, u32[]{:S(2)}, u32[]{:S(2)}) async-start(bf16[32,32,128]{2,1,0:T(8,128)(2,1)} %shard_map.207), calls=%async_computation.4 | async-start | bytes 524288 | tf_op jit(solution)/shard_map/all_to_all | solution.py:479
  134.9 23.2 %copy-start.15 = (bf16[384,128]{1,0:T(8,128)(2,1)S(1)}, bf16[384,128]{1,0:T(8,128)(2,1)}, u32[]{:S(2)}) copy-start(bf16[384,128]{1,0:T(8,128)(2,1)} %copy-done.14) | copy-start | bytes 294916
  134.9 23.6 %copy-start.13 = (bf16[384,128]{1,0:T(8,128)(2,1)S(1)}, bf16[384,128]{1,0:T(8,128)(2,1)}, u32[]{:S(2)}) copy-start(bf16[384,128]{1,0:T(8,128)(2,1)} %copy-done.12) | copy-start | bytes 294916
  134.9 25.9 %copy-start.11 = (bf16[384,128]{1,0:T(8,128)(2,1)S(1)}, bf16[384,128]{1,0:T(8,128)(2,1)}, u32[]{:S(2)}) copy-start(bf16[384,128]{1,0:T(8,128)(2,1)} %copy-done.10) | copy-start | bytes 294916
  134.9 29.9 %copy-start.21 = (bf16[384,128]{1,0:T(8,128)(2,1)S(1)}, bf16[384,128]{1,0:T(8,128)(2,1)}, u32[]{:S(2)}) copy-start(bf16[384,128]{1,0:T(8,128)(2,1)} %copy-done.20) | copy-start | bytes 294916
  135.0 13.2 %collective-permute-start.12 = (bf16[32,48,128]{2,1,0:T(8,128)(2,1)S(1)}, bf16[32,48,128]{2,1,0:T(8,128)(2,1)S(1)}, u32[]{:S(2)}, u32[]{:S(2)}) collective-permute-start(bf16[32,48,128]{2,1,0:T(8,128)(2,1)S(1)} %get-tuple-element.78), channel_id=1, source_target_pairs={{0,1},{1,2},{2,3},{3,0},{4,5},{5,6},{6,7},{7,4},{8,9},{9,10},{10,1... | collective-permute-start | bytes 1179656 | tf_op jit(solution)/shard_map/ppermute | solution.py:53
  136.3 11.9 %collective-permute-start.13 = (bf16[32,48,128]{2,1,0:T(8,128)(2,1)S(1)}, bf16[32,48,128]{2,1,0:T(8,128)(2,1)S(1)}, u32[]{:S(2)}, u32[]{:S(2)}) collective-permute-start(bf16[32,48,128]{2,1,0:T(8,128)(2,1)S(1)} %get-tuple-element.79), channel_id=1, source_target_pairs={{0,3},{1,0},{2,1},{3,2},{4,7},{5,4},{6,5},{7,6},{8,11},{9,8},{10,9... | collective-permute-start | bytes 1179656 | tf_op jit(solution)/shard_map/ppermute | solution.py:53
  149.2 19.2 %all-to-all-start.3 = ((bf16[32,48,128]{2,1,0:T(8,128)(2,1)}), bf16[32,48,128]{2,1,0:T(8,128)(2,1)S(1)}, u32[]{:S(2)}, u32[]{:S(2)}) async-start(bf16[32,48,128]{2,1,0:T(8,128)(2,1)} %shard_map.204), calls=%async_computation.3 | async-start | bytes 786432 | tf_op jit(solution)/shard_map/all_to_all | solution.py:479
  158.1 5.8 %collective-permute-start.6 = (bf16[384,128]{1,0:T(8,128)(2,1)S(1)}, bf16[384,128]{1,0:T(8,128)(2,1)S(1)}, u32[]{:S(2)}, u32[]{:S(2)}) collective-permute-start(bf16[384,128]{1,0:T(8,128)(2,1)S(1)} %copy-done.15), channel_id=1, source_target_pairs={{0,1},{1,2},{2,3},{3,0},{4,5},{5,6},{6,7},{7,4},{8,9},{9,10},{10,1... | collective-permute-start | bytes 294920 | tf_op jit(solution)/shard_map/ppermute | solution.py:53
  158.5 5.4 %collective-permute-start.7 = (bf16[384,128]{1,0:T(8,128)(2,1)S(1)}, bf16[384,128]{1,0:T(8,128)(2,1)S(1)}, u32[]{:S(2)}, u32[]{:S(2)}) collective-permute-start(bf16[384,128]{1,0:T(8,128)(2,1)S(1)} %copy-done.13), channel_id=1, source_target_pairs={{0,2},{1,3},{2,0},{3,1},{4,6},{5,7},{6,4},{7,5},{8,10},{9,11},{10,... | collective-permute-start | bytes 294920 | tf_op jit(solution)/shard_map/ppermute | solution.py:53
  160.8 4.0 %collective-permute-start.8 = (bf16[384,128]{1,0:T(8,128)(2,1)S(1)}, bf16[384,128]{1,0:T(8,128)(2,1)S(1)}, u32[]{:S(2)}, u32[]{:S(2)}) collective-permute-start(bf16[384,128]{1,0:T(8,128)(2,1)S(1)} %copy-done.11), channel_id=1, source_target_pairs={{0,3},{1,0},{2,1},{3,2},{4,7},{5,4},{6,5},{7,6},{8,11},{9,8},{10,9... | collective-permute-start | bytes 294920 | tf_op jit(solution)/shard_map/ppermute | solution.py:53
  167.0 14.5 %copy-start.7 = (s32[64,1,32]{2,1,0:T(1,128)S(1)}, s32[64,1,32]{2,1,0:T(1,128)}, u32[]{:S(2)}) copy-start(s32[64,1,32]{2,1,0:T(1,128)} %copy-done.6) | copy-start | bytes 24580
  168.4 35.6 %all-to-all-start.2 = ((bf16[64,48,128]{2,1,0:T(8,128)(2,1)}), bf16[64,48,128]{2,1,0:T(8,128)(2,1)S(1)}, u32[]{:S(2)}, u32[]{:S(2)}) async-start(bf16[64,48,128]{2,1,0:T(8,128)(2,1)} %shard_map.199), calls=%async_computation.2 | async-start | bytes 1572864 | tf_op jit(solution)/shard_map/all_to_all | solution.py:479
  183.0 25.0 %collective-permute-start.19 = (bf16[80,128]{1,0:T(8,128)(2,1)S(1)}, bf16[80,128]{1,0:T(8,128)(2,1)S(1)}, u32[]{:S(2)}, u32[]{:S(2)}) collective-permute-start(bf16[80,128]{1,0:T(8,128)(2,1)S(1)} %shard_map.208.a_ref), channel_id=1, source_target_pairs={{0,1},{1,2},{2,3},{3,0},{4,5},{5,6},{6,7},{7,4},{8,9},{9,10},{10,1... | collective-permute-start | bytes 61448 | tf_op jit(solution)/shard_map/ppermute | solution.py:53
  183.9 24.1 %collective-permute-start.20 = (bf16[80,128]{1,0:T(8,128)(2,1)S(1)}, bf16[80,128]{1,0:T(8,128)(2,1)S(1)}, u32[]{:S(2)}, u32[]{:S(2)}) collective-permute-start(bf16[80,128]{1,0:T(8,128)(2,1)S(1)} %shard_map.208.a_ref), channel_id=1, source_target_pairs={{0,2},{1,3},{2,0},{3,1},{4,6},{5,7},{6,4},{7,5},{8,10},{9,11},{10,... | collective-permute-start | bytes 61448 | tf_op jit(solution)/shard_map/ppermute | solution.py:53
  186.4 21.6 %collective-permute-start.21 = (bf16[80,128]{1,0:T(8,128)(2,1)S(1)}, bf16[80,128]{1,0:T(8,128)(2,1)S(1)}, u32[]{:S(2)}, u32[]{:S(2)}) collective-permute-start(bf16[80,128]{1,0:T(8,128)(2,1)S(1)} %shard_map.208.a_ref), channel_id=1, source_target_pairs={{0,3},{1,0},{2,1},{3,2},{4,7},{5,4},{6,5},{7,6},{8,11},{9,8},{10,9... | collective-permute-start | bytes 61448 | tf_op jit(solution)/shard_map/ppermute | solution.py:53
